TPU v7x, 32 devices: a whole 2x2x4 slice. The times are simulated.
32 devices in a mesh: rows: 4 (over x, core), hidden: 8 (over z, y).
Axes of the slice: x: 2, y: 2, z: 4, core: 2. Of those that a mesh axis runs over, the one named last changes fastest.
Arguments:
- resid_stream: bfloat16 [1024, 3584], P('rows'), may hold values from -6 to 6
- pre_gain: float32 [3584], replicated, may hold values from -0.5 to 0.5
- w_gate: bfloat16 [3584, 14336], P(None, 'hidden'), may hold values from -0.09375 to 0.09375
- w_up: bfloat16 [3584, 14336], P(None, 'hidden'), may hold values from -0.09375 to 0.09375
- w_down: bfloat16 [14336, 3584], P('hidden'), may hold values from -0.0625 to 0.0625
- w_enc: bfloat16 [3584, 8192], P(None, ('rows', 'hidden')), may hold values from -0.09375 to 0.09375
- b_enc: bfloat16 [8192], P(('rows', 'hidden')), may hold values from -3 to 3
- w_dec: bfloat16 [8192, 3584], P(('rows', 'hidden')), may hold values from -0.0625 to 0.0625
- b_dec: float32 [3584], replicated, may hold values from -3 to 3
Outputs:
- enc_grad: float32 [3584, 8192], P(None, ('rows', 'hidden'))
- dec_grad: float32 [8192, 3584], P(('rows', 'hidden'))
All inputs are finite; a program needn't handle non-finite values.
Results may differ from a plain program's by a relative error of at most 0.0062.
Values may be sent and summed in bfloat16 or wider, within the bound.
A program may use at most 128 MiB of HBM per device.

v0:
```python
import math

import jax
import jax.numpy as jnp
from jax import lax
from jax.sharding import PartitionSpec as P


def normed(resid_stream, pre_gain):
    values = resid_stream.astype(jnp.float32)
    variance = jnp.mean(values * values, axis=-1, keepdims=True)
    return (values * lax.rsqrt(variance + 1e-06) * (1.0 + pre_gain)).astype(jnp.bfloat16)


def contract_first(left, right):
    return lax.dot_general(
        left, right, (((0,), (0,)), ((), ())), preferred_element_type=jnp.float32
    )


def contract_last(left, right):
    return lax.dot_general(
        left, right, (((1,), (1,)), ((), ())), preferred_element_type=jnp.float32
    )


def on_device(resid_stream, pre_gain, w_gate, w_up, w_down, w_enc, b_enc, w_dec, b_dec):
    normal_in = normed(resid_stream, pre_gain)
    gate_proj = jnp.dot(normal_in, w_gate, preferred_element_type=jnp.float32)
    up_proj = jnp.dot(normal_in, w_up, preferred_element_type=jnp.float32)
    hidden_units = (jax.nn.gelu(gate_proj, approximate=True) * up_proj).astype(jnp.bfloat16)
    token_total = normal_in.shape[0] * lax.axis_size("rows")
    factor = 1.0 / math.sqrt(token_total)
    target = lax.psum_scatter(
        jnp.dot(hidden_units, w_down, preferred_element_type=jnp.float32),
        "hidden",
        scatter_dimension=1,
        tiled=True,
    )
    pre_act = jnp.dot(
        normal_in,
        lax.all_gather(w_enc, "rows", axis=1, tiled=True),
        preferred_element_type=jnp.float32,
    )
    dec_all, bias_all = (
        lax.all_gather(w_dec, "rows", axis=0, tiled=True),
        lax.all_gather(b_enc, "rows", axis=0, tiled=True),
    )
    pre_act = pre_act + bias_all.astype(jnp.float32)
    rectified = jnp.maximum(pre_act, 0.0)
    latent = (rectified * rectified).astype(jnp.bfloat16)
    recon = lax.psum_scatter(
        jnp.dot(latent, dec_all, preferred_element_type=jnp.float32),
        "hidden",
        scatter_dimension=1,
        tiled=True,
    )
    col_width = recon.shape[1]
    bias_part = lax.dynamic_slice_in_dim(b_dec, lax.axis_index("hidden") * col_width, col_width, 0)
    misfit = (recon + bias_part - target).astype(jnp.bfloat16)
    misfit_all = lax.all_gather(misfit, "hidden", axis=1, tiled=True)
    mis_rows = lax.all_gather(misfit_all, "rows", axis=0, tiled=True)
    tok_rows = lax.all_gather(normal_in, "rows", axis=0, tiled=True)
    own_pre = jnp.dot(tok_rows, w_enc, preferred_element_type=jnp.float32) + b_enc.astype(
        jnp.float32
    )
    own_rect = jnp.maximum(own_pre, 0.0)
    own_latent = (own_rect * own_rect).astype(jnp.bfloat16)
    dec_total = contract_first(own_latent, mis_rows)
    own_slope = (contract_last(mis_rows, w_dec) * 2.0 * own_rect).astype(jnp.bfloat16)
    enc_total = contract_first(tok_rows, own_slope)
    dec_total, enc_total = (dec_total, enc_total)
    return (enc_total * factor, dec_total * factor)


def solution(mesh):
    return jax.shard_map(
        on_device,
        mesh=mesh,
        in_specs=(
            P("rows", None),
            P(),
            P(None, "hidden"),
            P(None, "hidden"),
            P("hidden", None),
            P(None, ("rows", "hidden")),
            P(("rows", "hidden")),
            P(("rows", "hidden"), None),
            P(),
        ),
        out_specs=(P(None, ("rows", "hidden")), P(("rows", "hidden"), None)),
        check_vma=False,
    )
```

profile of v0, /device:TPU:0, one launch (start us, length us, event | category | flops | bytes accessed | tf_op | source)
XLA Modules:
  0.0 389.8 jit_solution(5063818987801974247)
XLA Ops:
  8.0 0.0 copy-start.1
  8.0 0.0 copy-start.3
  8.0 0.0 all-gather.9.cloned.1.call-start
  8.1 0.7 all-gather.9.cloned.1.call-update
  8.8 0.0 all-gather.11.cloned.1.call-start
  8.8 0.7 all-gather.11.cloned.1.call-update
  9.5 0.0 reduce-scatter.5.cloned.1.call-start
  9.6 0.0 copy-done.1
  9.6 0.4 fusion
  10.0 0.0 copy-done.3
  10.0 2.0 fusion.2
  12.1 0.0 copy-start
  12.1 8.4 %fusion.26 = f32[256,1792]{1,0:T(8,128)} fusion(bf16[256,3584]{1,0:T(8,128)(2,1)S(1)} %fusion.2, bf16[3584,1792]{1,0:T(8,128)(2,1)} %param.11), kind=kOutput, calls=%fused_computation.39 | convolution fusion | flops 3288334336 | bytes 16515072 | tf_op jit(solution)/shard_map/dot_general | solution.py:29
  20.5 16.4 %fusion.17 = f32[256,3584]{0,1:T(8,128)} fusion(bf16[1792,3584]{1,0:T(8,128)(2,1)} %param.13, bf16[256,3584]{1,0:T(8,128)(2,1)S(1)} %fusion.2, bf16[3584,1792]{1,0:T(8,128)(2,1)} %param.12, f32[256,1792]{1,0:T(8,128)} %fusion.26), kind=kOutput, calls=%fused_computation.27 | convolution fusion | flops 6581256192 | bytes 33030144 | tf_op jit(solution)/shard_map/dot_general | solution.py:35
  36.9 0.0 copy-start.6
  36.9 0.0 reduce-scatter.5.cloned.1.call-update
  36.9 0.0 reduce-scatter.3.cloned.1.call-start
  37.0 0.6 copy-done.6
  37.6 5.7 %all-gather = bf16[4,1,256]{2,1,0:T(2,128)(2,1)S(1)} all-gather(bf16[1,1,256]{2,1,0:T(2,128)(2,1)S(1)} %reshape.16), channel_id=1, replica_groups=mesh['rows'=4,'hidden'=8] {'rows'}, dimensions={0}, use_global_device_ids=true | all-gather | bytes 2560 | tf_op jit(solution)/shard_map/all_gather | solution.py:47
  43.3 23.2 %all-gather.9.cloned.1.call-done = bf16[3584,1024]{1,0:T(8,128)(2,1)} async-done(((bf16[3584,256]{1,0:T(8,128)(2,1)}), bf16[3584,1024]{1,0:T(8,128)(2,1)}) %all-gather.9.cloned.1.call-update) | async-done | bytes 7340048 | tf_op jit(solution)/shard_map/all_gather | solution.py:42
  66.5 54.0 %all-gather.11.cloned.1.call-done = bf16[1024,3584]{1,0:T(8,128)(2,1)} async-done(((bf16[256,3584]{1,0:T(8,128)(2,1)}), bf16[1024,3584]{1,0:T(8,128)(2,1)}) %all-gather.11.cloned.1.call-update) | async-done | bytes 7340048 | tf_op jit(solution)/shard_map/all_gather | solution.py:46
  120.4 0.0 copy-done
  120.4 11.1 %fusion.18 = f32[256,3584]{0,1:T(8,128)} fusion(bf16[1024,3584]{1,0:T(8,128)(2,1)} %all-gather.11.cloned.1.call-done, bf16[256,3584]{1,0:T(8,128)(2,1)S(1)} %fusion.2, bf16[3584,1024]{1,0:T(8,128)(2,1)} %all-gather.9.cloned.1.call-done, f32[1024]{0:T(1024)S(1)} %bitcast.16), kind=kOutput, calls=%fused_computation.28 | convolution fusion | flops 3759144960 | bytes 20189184 | tf_op jit(solution)/shard_map/dot_general | solution.py:53
  131.6 0.0 copy-start.2
  131.6 0.0 reduce-scatter.3.cloned.1.call-update
  131.6 0.0 all-gather.13.cloned.1.call-start
  131.6 0.9 dynamic_slice.3
  132.5 0.0 reduce-scatter.5.cloned.1.call-done
  132.5 79.8 %reduce-scatter.3.cloned.1.call-done = f32[256,448]{0,1:T(8,128)} async-done(((f32[256,3584]{0,1:T(8,128)}), f32[256,448]{0,1:T(8,128)}) %reduce-scatter.3.cloned.1.call-update) | async-done | bytes 458768 | tf_op jit(solution)/shard_map/reduce_scatter | solution.py:52
  212.3 2.0 subtract_convert_fusion
  214.3 0.0 all-gather.13.cloned.1.call-update
  214.3 0.0 all-gather.7.cloned.1.call-start
  214.4 0.7 all-gather.7.cloned.1.call-update
  215.1 0.2 all-gather.15.cloned.1.call-start
  215.3 45.8 %all-gather.13.cloned.1.call-done = bf16[256,3584]{0,1:T(8,128)(2,1)} async-done(((bf16[256,448]{0,1:T(8,128)(2,1)}), bf16[256,3584]{0,1:T(8,128)(2,1)}) %all-gather.13.cloned.1.call-update) | async-done | bytes 1835024 | tf_op jit(solution)/shard_map/all_gather | solution.py:61
  261.1 0.0 all-gather.15.cloned.1.call-update
  261.1 52.4 %all-gather.7.cloned.1.call-done = bf16[1024,3584]{1,0:T(8,128)(2,1)} async-done(((bf16[256,3584]{1,0:T(8,128)(2,1)}), bf16[1024,3584]{1,0:T(8,128)(2,1)}) %all-gather.7.cloned.1.call-update) | async-done | bytes 7340048 | tf_op jit(solution)/shard_map/all_gather | solution.py:63
  313.5 0.0 copy-done.2
  313.5 5.1 %fusion.12 = f32[1024,256]{1,0:T(8,128)S(1)} fusion(bf16[1024,3584]{1,0:T(8,128)(2,1)} %all-gather.7.cloned.1.call-done, bf16[3584,256]{1,0:T(8,128)(2,1)S(1)} %copy-done.2, f32[256]{0:T(256)S(1)} %convert_element_type.33), kind=kOutput, calls=%fused_computation.20 | convolution fusion | flops 1879572480 | bytes 10224640 | tf_op jit(solution)/shard_map/dot_general | solution.py:64
  318.7 49.6 %all-gather.15.cloned.1.call-done = bf16[1024,3584]{0,1:T(8,128)(2,1)} async-done(((bf16[256,3584]{0,1:T(8,128)(2,1)}), bf16[1024,3584]{0,1:T(8,128)(2,1)}) %all-gather.15.cloned.1.call-update) | async-done | bytes 7340048 | tf_op jit(solution)/shard_map/all_gather | solution.py:62
  368.3 0.0 copy-start.5
  368.3 5.9 %fusion.16 = bf16[1024,256]{1,0:T(8,128)(2,1)S(1)} fusion(f32[1024,256]{1,0:T(8,128)S(1)} %fusion.12, bf16[1024,3584]{0,1:T(8,128)(2,1)} %all-gather.15.cloned.1.call-done, bf16[256,3584]{1,0:T(8,128)(2,1)} %param.16), kind=kOutput, calls=%fused_computation.25 | convolution fusion | flops 1879834624 | bytes 10747904 | tf_op jit(solution)/shard_map/dot_general | solution.py:22
  374.1 0.0 copy-done.5
  374.1 0.0 copy-start.4
  374.1 4.0 %convolution_multiply_fusion = f32[256,3584]{1,0:T(8,128)} fusion(bf16[1024,3584]{0,1:T(8,128)(2,1)S(1)} %copy-done.5, f32[1024,256]{1,0:T(8,128)S(1)} %fusion.12), kind=kOutput, calls=%fused_computation | convolution fusion | flops 1880489984 | bytes 12058624 | tf_op jit(solution)/shard_map/dot_general | solution.py:16
  378.2 0.0 copy-done.4
  378.2 4.1 %convolution_multiply_fusion.1 = f32[3584,256]{1,0:T(8,128)} fusion(bf16[1024,3584]{1,0:T(8,128)(2,1)S(1)} %copy-done.4, bf16[1024,256]{1,0:T(8,128)(2,1)S(1)} %fusion.16), kind=kOutput, calls=%fused_computation.1 | convolution fusion | flops 1879965696 | bytes 11534336 | tf_op jit(solution)/shard_map/dot_general | solution.py:16
  (5 shorter events, 0.0 us)
Async XLA Ops:
  8.0 1.6 copy-start.1
  8.0 2.0 copy-start.3
  8.0 58.5 %all-gather.9.cloned.1.call-start = ((), (), s32[]{:S(2)}) async-start(), calls=%async_computation.3 | async-start | bytes 9175040 | tf_op jit(solution)/shard_map/all_gather | solution.py:42
  8.8 111.7 %all-gather.11.cloned.1.call-start = ((), (), s32[]{:S(2)}) async-start(), calls=%async_computation.4 | async-start | bytes 9175040 | tf_op jit(solution)/shard_map/all_gather | solution.py:46
  9.5 123.0 %reduce-scatter.5.cloned.1.call-start = ((), (), s32[]{:S(2)}) async-start(), calls=%async_computation.6 | async-start | bytes 4128768 | tf_op jit(solution)/shard_map/reduce_scatter | solution.py:34
  12.1 108.4 %copy-start = (bf16[256,3584]{1,0:T(8,128)(2,1)}, bf16[256,3584]{1,0:T(8,128)(2,1)S(1)}, u32[]{:S(2)}) copy-start(bf16[256,3584]{1,0:T(8,128)(2,1)S(1)} %fusion.2) | copy-start | bytes 5505028
  36.9 0.7 copy-start.6
  36.9 175.4 %reduce-scatter.3.cloned.1.call-start = ((), (), s32[]{:S(2)}) async-start(), calls=%async_computation.5 | async-start | bytes 4128768 | tf_op jit(solution)/shard_map/reduce_scatter | solution.py:52
  131.6 181.9 %copy-start.2 = (bf16[3584,256]{1,0:T(8,128)(2,1)S(1)}, bf16[3584,256]{1,0:T(8,128)(2,1)}, u32[]{:S(2)}) copy-start(bf16[3584,256]{1,0:T(8,128)(2,1)} %param.14) | copy-start | bytes 5505028
  131.6 129.5 %all-gather.13.cloned.1.call-start = ((), (), s32[]{:S(2)}) async-start(), calls=%async_computation.7 | async-start | bytes 2064384 | tf_op jit(solution)/shard_map/all_gather | solution.py:61
  214.3 99.2 %all-gather.7.cloned.1.call-start = ((), (), s32[]{:S(2)}) async-start(), calls=%async_computation.2 | async-start | bytes 9175040 | tf_op jit(solution)/shard_map/all_gather | solution.py:63
  215.1 153.2 %all-gather.15.cloned.1.call-start = ((), (), s32[]{:S(2)}) async-start(), calls=%async_computation.8 | async-start | bytes 9175040 | tf_op jit(solution)/shard_map/all_gather | solution.py:62
  368.3 5.9 %copy-start.5 = (bf16[1024,3584]{0,1:T(8,128)(2,1)S(1)}, bf16[1024,3584]{0,1:T(8,128)(2,1)}, u32[]{:S(2)}) copy-start(bf16[1024,3584]{0,1:T(8,128)(2,1)} %all-gather.15.cloned.1.call-done) | copy-start | bytes 22020100
  374.1 4.0 %copy-start.4 = (bf16[1024,3584]{1,0:T(8,128)(2,1)S(1)}, bf16[1024,3584]{1,0:T(8,128)(2,1)}, u32[]{:S(2)}) copy-start(bf16[1024,3584]{1,0:T(8,128)(2,1)} %all-gather.7.cloned.1.call-done) | copy-start | bytes 22020100
Sparse Core Ops, SparseCore 0:
  10.4 56.0 all-gather.8
  68.0 52.3 all-gather.10
Sparse Core Ops, SparseCore 1:
  37.0 82.9 reduce-scatter.4
  131.7 80.6 reduce-scatter.2
  215.0 46.1 all-gather.12
  262.7 50.7 all-gather.6
  315.1 53.1 all-gather.14
where the time goes:
time: 390 us
  waiting for transfers between devices  307 us (79%)
  matrix products  55.1 us (14%)
  between operations  15.8 us (4%)
  blocking collectives  5.67 us (1%)
  other arithmetic  4.45 us (1%)
    reduce_scatter x1, waiting for transfers between devices, on_device(): lax.psum_scatter(jnp.dot(latent, dec_all, preferred_element_type=jnp.floa...  79.8 us
    all_gather x1, waiting for transfers between devices, on_device(): lax.all_gather(w_dec, 'rows', axis=0, tiled=True)  54 us
    all_gather x1, waiting for transfers between devices, on_device(): tok_rows = lax.all_gather(normal_in, 'rows', axis=0, tiled=True)  52.4 us
    all_gather x1, waiting for transfers between devices, on_device(): mis_rows = lax.all_gather(misfit_all, 'rows', axis=0, tiled=True)  49.6 us
    all_gather x1, waiting for transfers between devices, on_device(): misfit_all = lax.all_gather(misfit, 'hidden', axis=1, tiled=True)  45.8 us
    all_gather x1, waiting for transfers between devices, on_device(): lax.all_gather(w_enc, 'rows', axis=1, tiled=True)  23.2 us
    dot_general x1, matrix products, on_device(): jnp.dot(hidden_units, w_down, preferred_element_type=jnp.float32)  16.4 us
    dot_general x1, matrix products, on_device(): jnp.dot(latent, dec_all, preferred_element_type=jnp.float32)  11.1 us
  transfers between devices with their start and end apart: 7, of which 6 were waited for; matrix products, arithmetic and copies ran while one was open for 11% of the time, Pallas kernels for 0%

commit v1 on v0

v1 whole, which is shorter than its diff:
```python
import functools
import math

import jax
import jax.numpy as jnp
from jax import lax
from jax.experimental import pallas as pl
from jax.experimental.pallas import tpu as pltpu
from jax.sharding import PartitionSpec as P

LANES = 128


def normed(resid_stream, pre_gain):
    values = resid_stream.astype(jnp.float32)
    variance = jnp.mean(values * values, axis=-1, keepdims=True)
    return (values * lax.rsqrt(variance + 1e-06) * (1.0 + pre_gain)).astype(jnp.bfloat16)


def contract_first(left, right):
    return lax.dot_general(
        left, right, (((0,), (0,)), ((), ())), preferred_element_type=jnp.float32
    )


def contract_last(left, right):
    return lax.dot_general(
        left, right, (((1,), (1,)), ((), ())), preferred_element_type=jnp.float32
    )


def by_rows(count, block, body):
    def step(i, carry):
        body(pl.multiple_of(i * block, block))
        return carry

    lax.fori_loop(0, count // block, step, 0)


def groups_of(half, count=4):
    tiles = half // LANES
    out, at = [], 0
    for i in range(count):
        width = (tiles // count + (1 if i < tiles % count else 0)) * LANES
        out.append((at, width))
        at += width
    return out


def total_kernel(
    z_size, part_ref, bias_ref, out_ref,
    core_in, acc0, in1, acc1, in2, acc2, in3, send_sem, recv_sem,
):
    tokens, features = part_ref.shape
    half_f = features // 2
    groups = groups_of(half_f)
    row, hid = lax.axis_index("rows"), lax.axis_index("hidden")
    x, core = row // 2, row % 2
    z, y = hid // 2, hid % 2
    core_peer = {"rows": x * 2 + (1 - core), "hidden": hid}
    x_peer = {"rows": (1 - x) * 2 + core, "hidden": hid}
    y_peer = {"rows": row, "hidden": z * 2 + (1 - y)}
    z_peers = [
        {"rows": row, "hidden": lax.rem(z + d, z_size) * 2 + y} for d in range(1, z_size)
    ]
    stages = 2 * (3 + z_size - 1)

    barrier = pltpu.get_barrier_semaphore()
    peers = [core_peer, x_peer, y_peer] + z_peers
    for peer in peers:
        pl.semaphore_signal(barrier, inc=1, device_id=peer, device_id_type=pl.DeviceIdType.MESH)
    pl.semaphore_wait(barrier, len(peers))

    def copy(group, stage, src, dst, peer):
        at = group * stages + stage
        return pltpu.make_async_remote_copy(
            src_ref=src, dst_ref=dst, send_sem=send_sem.at[at], recv_sem=recv_sem.at[at],
            device_id=peer, device_id_type=pl.DeviceIdType.MESH,
        )

    t1, t2, t3 = tokens // 2, tokens // 4, tokens // (4 * z_size)
    started = []

    def go(copies):
        for c in copies:
            c.start()
        started.extend(copies)
        return copies

    def mine(off, width):
        return pl.ds(pl.multiple_of(core * half_f + off, LANES), width)

    def rows_at(start, size):
        return pl.ds(pl.multiple_of(start, size), size)

    def bits(g):
        return (x, y, x_peer, y_peer) if g % 2 == 0 else (y, x, y_peer, x_peer)

    flying = []
    for g, (off, width) in enumerate(groups):
        theirs = pl.ds(pl.multiple_of((1 - core) * half_f + off, LANES), width)
        flying.append(go([copy(g, 0, part_ref.at[:, theirs], core_in.at[:, pl.ds(off, width)], core_peer)]))

    for g, (off, width) in enumerate(groups):
        b1, b2, p1, p2 = bits(g)
        cols, own = pl.ds(off, width), mine(off, width)
        flying[g][0].wait_recv()

        def add0(i):
            rows = pl.ds(i, 32)
            acc0[rows, cols] = (
                part_ref[rows, own].astype(jnp.float32) + core_in[rows, cols].astype(jnp.float32)
            ).astype(jnp.bfloat16)

        by_rows(tokens, 32, add0)
        flying[g] = go([copy(g, 1, acc0.at[rows_at((1 - b1) * t1, t1), cols], in1.at[:, cols], p1)])

    for g, (off, width) in enumerate(groups):
        b1, b2, p1, p2 = bits(g)
        cols = pl.ds(off, width)
        flying[g][0].wait_recv()

        def add1(i):
            rows = pl.ds(i, 32)
            kept = pl.ds(pl.multiple_of(b1 * t1 + i, 32), 32)
            acc1[rows, cols] = (
                acc0[kept, cols].astype(jnp.float32) + in1[rows, cols].astype(jnp.float32)
            ).astype(jnp.bfloat16)

        by_rows(t1, 32, add1)
        flying[g] = go([copy(g, 2, acc1.at[rows_at((1 - b2) * t2, t2), cols], in2.at[:, cols], p2)])

    for g, (off, width) in enumerate(groups):
        b1, b2, p1, p2 = bits(g)
        cols = pl.ds(off, width)
        flying[g][0].wait_recv()

        def add2(i):
            rows = pl.ds(i, 32)
            kept = pl.ds(pl.multiple_of(b2 * t2 + i, 32), 32)
            acc2[rows, cols] = (
                acc1[kept, cols].astype(jnp.float32) + in2[rows, cols].astype(jnp.float32)
            ).astype(jnp.bfloat16)

        by_rows(t2, 32, add2)
        flying[g] = go([
            copy(g, 3 + d, acc2.at[rows_at(lax.rem(z + 1 + d, z_size) * t3, t3), cols],
                 in3.at[d, :, cols], z_peers[d])
            for d in range(z_size - 1)
        ])

    base = 3 + z_size - 1
    for g, (off, width) in enumerate(groups):
        b1, b2, p1, p2 = bits(g)
        cols, own = pl.ds(off, width), mine(off, width)
        for c in flying[g]:
            c.wait_recv()
        start = b1 * t1 + b2 * t2 + z * t3

        def add3(i):
            rows = pl.ds(i, 16)
            total = acc2[pl.ds(pl.multiple_of(z * t3 + i, 16), 16), cols].astype(jnp.float32)
            for d in range(z_size - 1):
                total = total + in3[d, rows, cols].astype(jnp.float32)
            total = total + bias_ref[:, own]
            out_ref[pl.ds(pl.multiple_of(start + i, 16), 16), own] = total.astype(jnp.bfloat16)

        by_rows(t3, 16, add3)
        block = out_ref.at[rows_at(start, t3), own]
        flying[g] = go([copy(g, base + d, block, block, z_peers[d]) for d in range(z_size - 1)])

    for g, (off, width) in enumerate(groups):
        b1, b2, p1, p2 = bits(g)
        for c in flying[g]:
            c.wait_recv()
        block = out_ref.at[rows_at(b1 * t1 + b2 * t2, t2), mine(off, width)]
        flying[g] = go([copy(g, base + z_size - 1, block, block, p2)])

    for g, (off, width) in enumerate(groups):
        b1, b2, p1, p2 = bits(g)
        flying[g][0].wait_recv()
        block = out_ref.at[rows_at(b1 * t1, t1), mine(off, width)]
        flying[g] = go([copy(g, base + z_size, block, block, p1)])

    for g, (off, width) in enumerate(groups):
        flying[g][0].wait_recv()
        block = out_ref.at[:, mine(off, width)]
        flying[g] = go([copy(g, base + z_size + 1, block, block, core_peer)])

    for g in range(len(groups)):
        flying[g][0].wait_recv()
    for c in started:
        c.wait_send()


def total_over_devices(part, bias, z_size):
    tokens, features = part.shape
    half_f = features // 2
    stages = 2 * (3 + z_size - 1) * len(groups_of(half_f))
    t1, t2, t3 = tokens // 2, tokens // 4, tokens // (4 * z_size)
    bf = jnp.bfloat16
    return pl.pallas_call(
        functools.partial(total_kernel, z_size),
        out_shape=jax.ShapeDtypeStruct((tokens, features), bf),
        in_specs=[pl.BlockSpec(memory_space=pltpu.VMEM)] * 2,
        out_specs=pl.BlockSpec(memory_space=pltpu.VMEM),
        scratch_shapes=[
            pltpu.VMEM((tokens, half_f), bf),
            pltpu.VMEM((tokens, half_f), bf),
            pltpu.VMEM((t1, half_f), bf),
            pltpu.VMEM((t1, half_f), bf),
            pltpu.VMEM((t2, half_f), bf),
            pltpu.VMEM((t2, half_f), bf),
            pltpu.VMEM((z_size - 1, t3, half_f), bf),
            pltpu.SemaphoreType.DMA((stages,)),
            pltpu.SemaphoreType.DMA((stages,)),
        ],
        compiler_params=pltpu.CompilerParams(
            collective_id=0, has_side_effects=True, vmem_limit_bytes=48 * 1024 * 1024
        ),
    )(part, bias)


def on_device(z_size, resid_stream, pre_gain, w_gate, w_up, w_down, w_enc, b_enc, w_dec, b_dec):
    normal_in = normed(resid_stream, pre_gain)
    tok_rows = lax.all_gather(normal_in, "rows", axis=0, tiled=True)
    gate_proj = jnp.dot(normal_in, w_gate, preferred_element_type=jnp.float32)
    up_proj = jnp.dot(normal_in, w_up, preferred_element_type=jnp.float32)
    hidden_units = (jax.nn.gelu(gate_proj, approximate=True) * up_proj).astype(jnp.bfloat16)
    target = jnp.dot(hidden_units, w_down, preferred_element_type=jnp.float32)

    row_size = lax.axis_size("rows")
    own_tokens, features = normal_in.shape
    factor = 1.0 / math.sqrt(own_tokens * row_size)
    own_pre = jnp.dot(tok_rows, w_enc, preferred_element_type=jnp.float32) + b_enc.astype(
        jnp.float32
    )
    own_rect = jnp.maximum(own_pre, 0.0)
    own_latent = (own_rect * own_rect).astype(jnp.bfloat16)
    recon = jnp.dot(own_latent, w_dec, preferred_element_type=jnp.float32)
    own_block = (jnp.arange(row_size) == lax.axis_index("rows"))[:, None, None]
    part = recon.reshape(row_size, own_tokens, features) - jnp.where(own_block, target[None], 0.0)
    part = part.reshape(row_size * own_tokens, features).astype(jnp.bfloat16)
    mis_rows = total_over_devices(part, b_dec.reshape(1, features), z_size)

    dec_total = contract_first(own_latent, mis_rows)
    own_slope = (contract_last(mis_rows, w_dec) * 2.0 * own_rect).astype(jnp.bfloat16)
    enc_total = contract_first(tok_rows, own_slope)
    return (enc_total * factor, dec_total * factor)


def solution(mesh):
    return jax.shard_map(
        functools.partial(on_device, mesh.shape["hidden"] // 2),
        mesh=mesh,
        in_specs=(
            P("rows", None),
            P(),
            P(None, "hidden"),
            P(None, "hidden"),
            P("hidden", None),
            P(None, ("rows", "hidden")),
            P(("rows", "hidden")),
            P(("rows", "hidden"), None),
            P(),
        ),
        out_specs=(P(None, ("rows", "hidden")), P(("rows", "hidden"), None)),
        check_vma=False,
    )
```

time: 390 us -> 210 us (0.54)
  waiting for transfers between devices: 307 us -> 24.7 us
  Pallas kernels: 0 us -> 110 us
  blocking collectives: 5.67 us -> 0 us
    all_gather x4 -> x0, waiting for transfers between devices: 173 us -> none  [the longest x1 54 us: on_device(): lax.all_gather(w_dec, 'rows', axis=0, tiled=True)]
    pallas_call x0 -> x1, Pallas kernels: none -> 110 us  [total_over_devices(): pl.pallas_call(functools.partial(total_kernel, z_size), out_shape=jax.Sha...]
    reduce_scatter x2 -> x0, waiting for transfers between devices: 79.8 us -> none  [the longest x1 79.8 us: on_device(): lax.psum_scatter(jnp.dot(latent, dec_all, preferred_element_type=jnp.floa...]
    all_gather x1, waiting for transfers between devices: 52.4 us -> 24.7 us  [on_device(): tok_rows = lax.all_gather(normal_in, 'rows', axis=0, tiled=True)]
    all_gather x1 -> x0, blocking collectives: 5.67 us -> none  [on_device(): lax.all_gather(b_enc, 'rows', axis=0, tiled=True)]
  transfers between devices with their start and end apart: 7 -> 1, of which waited for: 6 -> 1; matrix products, arithmetic and copies ran while one was open for 11% -> 15% of each run, Pallas kernels for 0% -> 0%
where the time goes in v1:
time: 210 us; the launch traced here: 209 us
  Pallas kernels  110 us (52%)
  matrix products  54.1 us (26%)
  waiting for transfers between devices  24.7 us (12%)
  between operations  14.2 us (7%)
  other arithmetic  6.04 us (3%)
    pallas_call x1, Pallas kernels, total_over_devices(): pl.pallas_call(functools.partial(total_kernel, z_size), out_shape=jax.Sha...  110 us
    all_gather x1, waiting for transfers between devices, on_device(): tok_rows = lax.all_gather(normal_in, 'rows', axis=0, tiled=True)  24.7 us
    dot_general x1, matrix products, on_device(): target = jnp.dot(hidden_units, w_down, preferred_element_type=jnp.float32)  20.4 us
    dot_general x1, matrix products, on_device(): gate_proj = jnp.dot(normal_in, w_gate, preferred_element_type=jnp.float32)  9.99 us
    dot_general x2, matrix products, contract_first(): lax.dot_general(left, right, (((0,), (0,)), ((), ())), preferred_element_...  7.89 us
    dot_general x1, matrix products, on_device(): jnp.dot(tok_rows, w_enc, preferred_element_type=jnp.float32)  5.79 us
    dot_general x1, matrix products, contract_last(): lax.dot_general(left, right, (((1,), (1,)), ((), ())), preferred_element_...  5.32 us
    dot_general x1, matrix products, on_device(): recon = jnp.dot(own_latent, w_dec, preferred_element_type=jnp.float32)  4.74 us
  transfers between devices with their start and end apart: 1, of which 1 were waited for; matrix products, arithmetic and copies ran while one was open for 15% of the time, Pallas kernels for 0%

profile of v1, /device:TPU:0, one launch (start us, length us, event | category | flops | bytes accessed | tf_op | source)
XLA Modules:
  0.0 209.4 jit_solution(8465959220663095118)
XLA Ops:
  7.2 0.0 copy-start
  7.2 0.0 copy-start.4
  7.2 0.0 copy-start.3
  7.2 0.0 all-gather.2.cloned.1.call-start
  7.2 2.1 fusion.2
  9.3 0.7 broadcast_add_fusion
  10.0 3.2 %fusion.4 = bf16[256,3584]{1,0:T(8,128)(2,1)} fusion(bf16[256,3584]{1,0:T(8,128)(2,1)} %param.9, f32[3584]{0:T(1024)S(1)} %broadcast_add_fusion, f32[256]{0:T(256)S(1)} %add_rsqrt_fusion), kind=kLoop, calls=%fused_computation.9 | loop fusion | flops 3670016 | bytes 3685376 | tf_op jit(solution)/shard_map/convert_element_type | solution.py:17
  13.3 0.0 all-gather.2.cloned.1.call-update
  13.3 0.1 broadcast_in_dim.31
  13.4 0.0 copy-done.4
  13.4 0.0 copy-done.3
  13.4 10.0 %fusion.21 = f32[256,1792]{1,0:T(8,128)} fusion(bf16[256,3584]{1,0:T(8,128)(2,1)} %fusion.4, bf16[3584,1792]{1,0:T(8,128)(2,1)} %param.11), kind=kOutput, calls=%fused_computation.34 | convolution fusion | flops 3288334336 | bytes 16515072 | tf_op jit(solution)/shard_map/dot_general | solution.py:227
  23.4 20.4 %fusion.16 = f32[256,3584]{1,0:T(8,128)} fusion(bf16[1792,3584]{1,0:T(8,128)(2,1)} %param.13, bf16[256,3584]{1,0:T(8,128)(2,1)} %fusion.4, bf16[3584,1792]{1,0:T(8,128)(2,1)} %param.12, f32[256,1792]{1,0:T(8,128)} %fusion.21), kind=kOutput, calls=%fused_computation.26 | convolution fusion | flops 6581256192 | bytes 33030144 | tf_op jit(solution)/shard_map/dot_general | solution.py:230
  43.8 24.7 %all-gather.2.cloned.1.call-done = bf16[1024,3584]{1,0:T(8,128)(2,1)} async-done(((bf16[256,3584]{1,0:T(8,128)(2,1)}), bf16[1024,3584]{1,0:T(8,128)(2,1)}) %all-gather.2.cloned.1.call-update) | async-done | bytes 7340048 | tf_op jit(solution)/shard_map/all_gather | solution.py:226
  68.5 0.0 copy-start.2
  68.5 5.8 %fusion.14 = f32[1024,256]{1,0:T(8,128)S(1)} fusion(bf16[1024,3584]{1,0:T(8,128)(2,1)} %all-gather.2.cloned.1.call-done, bf16[3584,256]{1,0:T(8,128)(2,1)} %param.14, f32[256]{0:T(256)S(1)} %convert_element_type.23), kind=kOutput, calls=%fused_computation.23 | convolution fusion | flops 1879572480 | bytes 10224640 | tf_op jit(solution)/shard_map/dot_general | solution.py:235
  74.3 0.0 copy-done
  74.3 0.0 copy-done.2
  74.3 4.7 %fusion.1.part_ref = bf16[1024,3584]{1,0:T(8,128)(2,1)} fusion(bf16[256,3584]{1,0:T(8,128)(2,1)S(1)} %copy-done, f32[256,3584]{1,0:T(8,128)S(1)} %copy-done.2, pred[1024]{0:T(1024)(128)(4,1)S(1)} %broadcast_in_dim.32, f32[1024,256]{1,0:T(8,128)S(1)} %fusion.14), kind=kOutput, calls=%fused_computation.2 | convolution fusion | flops 1890582528 | bytes 13894656 | tf_op jit(solution)/shard_map/dot_general | solution.py:240
  79.1 110.3 %shard_map.104 = bf16[1024,3584]{1,0:T(8,128)(2,1)} custom-call(bf16[1024,3584]{1,0:T(8,128)(2,1)} %fusion.1.part_ref, f32[1,3584]{1,0:T(1,128)S(1)} %reshape.26.bias_ref), custom_call_target="tpu_custom_call" | custom-call | tf_op jit(solution)/shard_map/pallas_call | solution.py:202
  189.3 0.0 copy-start.1
  189.3 0.0 slice-start
  189.3 5.3 %fusion.15 = bf16[1024,256]{1,0:T(8,128)(2,1)S(1)} fusion(f32[1024,256]{1,0:T(8,128)S(1)} %fusion.14, bf16[1024,3584]{1,0:T(8,128)(2,1)} %shard_map.104, bf16[256,3584]{1,0:T(8,128)(2,1)S(1)} %copy-done), kind=kOutput, calls=%fused_computation.24 | convolution fusion | flops 1879834624 | bytes 10747904 | tf_op jit(solution)/shard_map/dot_general | solution.py:27
  194.7 0.0 copy-done.1
  194.7 0.0 slice-start.1
  194.7 3.9 %convolution_multiply_fusion = f32[256,3584]{1,0:T(8,128)} fusion(bf16[1024,3584]{1,0:T(8,128)(2,1)S(1)} %copy-done.1, f32[1024,256]{1,0:T(8,128)S(1)} %fusion.14), kind=kOutput, calls=%fused_computation.3 | convolution fusion | flops 1880489984 | bytes 12058624 | tf_op jit(solution)/shard_map/dot_general | solution.py:21
  198.6 0.0 slice-done
  198.6 0.0 slice-done.1
  198.6 4.0 %convolution_multiply_fusion.1 = f32[3584,256]{1,0:T(8,128)} fusion(bf16[1024,3584]{1,0:T(8,128)(2,1)S(1)} %bitcast.20, bf16[1024,256]{1,0:T(8,128)(2,1)S(1)} %fusion.15), kind=kOutput, calls=%fused_computation.4 | convolution fusion | flops 1879965696 | bytes 11534336 | tf_op jit(solution)/shard_map/dot_general | solution.py:21
  (6 shorter events, 0.0 us)
Async XLA Ops:
  7.2 67.1 %copy-start = (bf16[256,3584]{1,0:T(8,128)(2,1)S(1)}, bf16[256,3584]{1,0:T(8,128)(2,1)}, u32[]{:S(2)}) copy-start(bf16[256,3584]{1,0:T(8,128)(2,1)} %param.16) | copy-start | bytes 5505028
  7.2 6.2 %copy-start.4 = (bf16[256]{0:T(256)(128)(2,1)S(1)}, bf16[256]{0:T(256)(128)(2,1)}, u32[]{:S(2)}) copy-start(bf16[256]{0:T(256)(128)(2,1)} %param.15) | copy-start | bytes 1540
  7.2 6.2 %copy-start.3 = (f32[3584]{0:T(1024)S(1)}, f32[3584]{0:T(1024)}, u32[]{:S(2)}) copy-start(f32[3584]{0:T(1024)} %param.17) | copy-start | bytes 43012
  7.2 61.3 %all-gather.2.cloned.1.call-start = ((), (), s32[]{:S(2)}) async-start(), calls=%async_computation | async-start | bytes 9175040 | tf_op jit(solution)/shard_map/all_gather | solution.py:226
  68.5 5.8 %copy-start.2 = (f32[256,3584]{1,0:T(8,128)S(1)}, f32[256,3584]{1,0:T(8,128)}, u32[]{:S(2)}) copy-start(f32[256,3584]{1,0:T(8,128)} %fusion.16) | copy-start | bytes 11010052
  189.3 5.3 %copy-start.1 = (bf16[1024,3584]{1,0:T(8,128)(2,1)S(1)}, bf16[1024,3584]{1,0:T(8,128)(2,1)}, u32[]{:S(2)}) copy-start(bf16[1024,3584]{1,0:T(8,128)(2,1)} %shard_map.104) | copy-start | bytes 22020100
  189.3 9.3 %slice-start = ((s8[7340032]{0:T(1024)(128)(4,1)}), s8[4194304]{0:T(1024)(128)(4,1)S(1)}, s32[]{:S(2)}) async-start(s8[7340032]{0:T(1024)(128)(4,1)} %bitcast.19), calls=%async_computation.1 | async-start | bytes 8388608
  194.7 3.9 %slice-start.1 = ((s8[7340032]{0:T(1024)(128)(4,1)}), s8[3145728]{0:T(1024)(128)(4,1)S(1)}, s32[]{:S(2)}) async-start(s8[7340032]{0:T(1024)(128)(4,1)} %bitcast.19), calls=%async_computation.2 | async-start | bytes 6291456
Sparse Core Ops, SparseCore 0:
  13.4 55.0 all-gather.1

commit v2 on v1

--- a/solution.py
+++ b/solution.py
@@ -37,14 +37,11 @@
     lax.fori_loop(0, count // block, step, 0)
 
 
-def groups_of(half, count=4):
-    tiles = half // LANES
-    out, at = [], 0
-    for i in range(count):
-        width = (tiles // count + (1 if i < tiles % count else 0)) * LANES
-        out.append((at, width))
-        at += width
-    return out
+def groups_of(half):
+    return [(at, LANES) for at in range(0, half, LANES)]
+
+
+LAGS = (0, 2, 3, 4, 5, 6, 8, 9)
 
 
 def total_kernel(
@@ -96,99 +93,100 @@
     def bits(g):
         return (x, y, x_peer, y_peer) if g % 2 == 0 else (y, x, y_peer, x_peer)
 
+    base = 3 + z_size - 1
     flying = []
     for g, (off, width) in enumerate(groups):
         theirs = pl.ds(pl.multiple_of((1 - core) * half_f + off, LANES), width)
         flying.append(go([copy(g, 0, part_ref.at[:, theirs], core_in.at[:, pl.ds(off, width)], core_peer)]))
 
-    for g, (off, width) in enumerate(groups):
+    def sum_cores(g):
+        off, width = groups[g]
         b1, b2, p1, p2 = bits(g)
         cols, own = pl.ds(off, width), mine(off, width)
-        flying[g][0].wait_recv()
-
-        def add0(i):
-            rows = pl.ds(i, 32)
+
+        def add(i):
+            rows = pl.ds(i, 128)
             acc0[rows, cols] = (
                 part_ref[rows, own].astype(jnp.float32) + core_in[rows, cols].astype(jnp.float32)
             ).astype(jnp.bfloat16)
 
-        by_rows(tokens, 32, add0)
-        flying[g] = go([copy(g, 1, acc0.at[rows_at((1 - b1) * t1, t1), cols], in1.at[:, cols], p1)])
-
-    for g, (off, width) in enumerate(groups):
+        by_rows(tokens, 128, add)
+        return [copy(g, 1, acc0.at[rows_at((1 - b1) * t1, t1), cols], in1.at[:, cols], p1)]
+
+    def sum_first(g):
+        off, width = groups[g]
         b1, b2, p1, p2 = bits(g)
         cols = pl.ds(off, width)
-        flying[g][0].wait_recv()
-
-        def add1(i):
-            rows = pl.ds(i, 32)
-            kept = pl.ds(pl.multiple_of(b1 * t1 + i, 32), 32)
+
+        def add(i):
+            kept = pl.ds(pl.multiple_of(b1 * t1 + i, 128), 128)
+            rows = pl.ds(i, 128)
             acc1[rows, cols] = (
                 acc0[kept, cols].astype(jnp.float32) + in1[rows, cols].astype(jnp.float32)
             ).astype(jnp.bfloat16)
 
-        by_rows(t1, 32, add1)
-        flying[g] = go([copy(g, 2, acc1.at[rows_at((1 - b2) * t2, t2), cols], in2.at[:, cols], p2)])
-
-    for g, (off, width) in enumerate(groups):
+        by_rows(t1, 128, add)
+        return [copy(g, 2, acc1.at[rows_at((1 - b2) * t2, t2), cols], in2.at[:, cols], p2)]
+
+    def sum_second(g):
+        off, width = groups[g]
         b1, b2, p1, p2 = bits(g)
         cols = pl.ds(off, width)
-        flying[g][0].wait_recv()
-
-        def add2(i):
-            rows = pl.ds(i, 32)
-            kept = pl.ds(pl.multiple_of(b2 * t2 + i, 32), 32)
+
+        def add(i):
+            kept = pl.ds(pl.multiple_of(b2 * t2 + i, 128), 128)
+            rows = pl.ds(i, 128)
             acc2[rows, cols] = (
                 acc1[kept, cols].astype(jnp.float32) + in2[rows, cols].astype(jnp.float32)
             ).astype(jnp.bfloat16)
 
-        by_rows(t2, 32, add2)
-        flying[g] = go([
+        by_rows(t2, 128, add)
+        return [
             copy(g, 3 + d, acc2.at[rows_at(lax.rem(z + 1 + d, z_size) * t3, t3), cols],
                  in3.at[d, :, cols], z_peers[d])
             for d in range(z_size - 1)
-        ])
-
-    base = 3 + z_size - 1
-    for g, (off, width) in enumerate(groups):
+        ]
+
+    def sum_last(g):
+        off, width = groups[g]
         b1, b2, p1, p2 = bits(g)
         cols, own = pl.ds(off, width), mine(off, width)
-        for c in flying[g]:
-            c.wait_recv()
         start = b1 * t1 + b2 * t2 + z * t3
-
-        def add3(i):
-            rows = pl.ds(i, 16)
-            total = acc2[pl.ds(pl.multiple_of(z * t3 + i, 16), 16), cols].astype(jnp.float32)
-            for d in range(z_size - 1):
-                total = total + in3[d, rows, cols].astype(jnp.float32)
-            total = total + bias_ref[:, own]
-            out_ref[pl.ds(pl.multiple_of(start + i, 16), 16), own] = total.astype(jnp.bfloat16)
-
-        by_rows(t3, 16, add3)
+        total = acc2[rows_at(z * t3, t3), cols].astype(jnp.float32)
+        for d in range(z_size - 1):
+            total = total + in3[d, :, cols].astype(jnp.float32)
+        out_ref[rows_at(start, t3), own] = (total + bias_ref[:, own]).astype(jnp.bfloat16)
         block = out_ref.at[rows_at(start, t3), own]
-        flying[g] = go([copy(g, base + d, block, block, z_peers[d]) for d in range(z_size - 1)])
-
-    for g, (off, width) in enumerate(groups):
-        b1, b2, p1, p2 = bits(g)
-        for c in flying[g]:
-            c.wait_recv()
-        block = out_ref.at[rows_at(b1 * t1 + b2 * t2, t2), mine(off, width)]
-        flying[g] = go([copy(g, base + z_size - 1, block, block, p2)])
-
-    for g, (off, width) in enumerate(groups):
-        b1, b2, p1, p2 = bits(g)
-        flying[g][0].wait_recv()
-        block = out_ref.at[rows_at(b1 * t1, t1), mine(off, width)]
-        flying[g] = go([copy(g, base + z_size, block, block, p1)])
-
-    for g, (off, width) in enumerate(groups):
-        flying[g][0].wait_recv()
-        block = out_ref.at[:, mine(off, width)]
-        flying[g] = go([copy(g, base + z_size + 1, block, block, core_peer)])
-
-    for g in range(len(groups)):
-        flying[g][0].wait_recv()
+        return [copy(g, base + d, block, block, z_peers[d]) for d in range(z_size - 1)]
+
+    def give_quarter(g):
+        b1, b2, p1, p2 = bits(g)
+        block = out_ref.at[rows_at(b1 * t1 + b2 * t2, t2), mine(*groups[g])]
+        return [copy(g, base + z_size - 1, block, block, p2)]
+
+    def give_half(g):
+        b1, b2, p1, p2 = bits(g)
+        block = out_ref.at[rows_at(b1 * t1, t1), mine(*groups[g])]
+        return [copy(g, base + z_size, block, block, p1)]
+
+    def give_core(g):
+        block = out_ref.at[:, mine(*groups[g])]
+        return [copy(g, base + z_size + 1, block, block, core_peer)]
+
+    def end(g):
+        return []
+
+    work = (sum_cores, sum_first, sum_second, sum_last, give_quarter, give_half, give_core, end)
+    count = len(groups)
+    for step in range((count + 1) // 2 + LAGS[-1]):
+        for stage in (0,) + tuple(range(len(work) - 1, 0, -1)):
+            pair = step - LAGS[stage]
+            for g in (2 * pair, 2 * pair + 1):
+                if 0 <= g < count:
+                    for c in flying[g]:
+                        c.wait_recv()
+                    flying[g] = go(work[stage](g))
+
     for c in started:
         c.wait_send()
 
@@ -221,9 +219,44 @@
     )(part, bias)
 
 
+def swap(values, axis, distance):
+    return lax.ppermute(values, axis, [(i, i ^ distance) for i in range(lax.axis_size(axis))])
+
+
+def gather_tokens(own):
+    count, features = own.shape
+    row, y = lax.axis_index("rows"), lax.axis_index("hidden") % 2
+    pieces = 2
+    size = count // (2 * pieces)
+    everyone = jnp.zeros((lax.axis_size("rows") * count, features), own.dtype)
+
+    def place(everyone, values, start):
+        return lax.dynamic_update_slice_in_dim(everyone, values, start, 0)
+
+    over_x = [
+        swap(lax.dynamic_slice_in_dim(own, y * (count // 2) + i * size, size, 0), "rows", 2)
+        for i in range(pieces)
+    ]
+    over_y = [swap(values, "hidden", 1) for values in over_x]
+    on_chip = swap(own, "rows", 1)
+    everyone = place(everyone, own, row * count)
+    everyone = place(everyone, on_chip, (row ^ 1) * count)
+    across = (row ^ 2) * count
+    far = [swap(values, "rows", 1) for values in over_x + over_y]
+    near_far = (row ^ 3) * count
+    for i in range(pieces):
+        here = y * (count // 2) + i * size
+        there = (1 - y) * (count // 2) + i * size
+        everyone = place(everyone, over_x[i], across + here)
+        everyone = place(everyone, over_y[i], across + there)
+        everyone = place(everyone, far[i], near_far + here)
+        everyone = place(everyone, far[pieces + i], near_far + there)
+    return everyone
+
+
 def on_device(z_size, resid_stream, pre_gain, w_gate, w_up, w_down, w_enc, b_enc, w_dec, b_dec):
     normal_in = normed(resid_stream, pre_gain)
-    tok_rows = lax.all_gather(normal_in, "rows", axis=0, tiled=True)
+    tok_rows = gather_tokens(normal_in)
     gate_proj = jnp.dot(normal_in, w_gate, preferred_element_type=jnp.float32)
     up_proj = jnp.dot(normal_in, w_up, preferred_element_type=jnp.float32)
     hidden_units = (jax.nn.gelu(gate_proj, approximate=True) * up_proj).astype(jnp.bfloat16)

time: 210 us -> 178 us (0.85)
  Pallas kernels: 110 us -> 84.5 us
  waiting for transfers between devices: 24.7 us -> 9.05 us
  local copies, waits for them, and re-layouts: 0.13 us -> 15.1 us
  between operations: 14.2 us -> 0.8 us
  starting transfers between devices: 0.04 us -> 7.93 us
    pallas_call x1, Pallas kernels: 110 us -> 84.5 us  [total_over_devices(): pl.pallas_call(functools.partial(total_kernel, z_size), out_shape=jax.Sha...]
    all_gather x1 -> x0, waiting for transfers between devices: 24.7 us -> none  [on_device(): tok_rows = lax.all_gather(normal_in, 'rows', axis=0, tiled=True)]
    dynamic_update_slice x0 -> x9, local copies, waits for them, and re-layouts: none -> 10.4 us  [place(): return lax.dynamic_update_slice_in_dim(everyone, values, start, 0)]
    ppermute x0 -> x9, waiting for transfers between devices: none -> 9.05 us  [swap(): lax.ppermute(values, axis, [(i, i ^ distance) for i in range(lax.axis_siz...]
    ppermute x0 -> x9, starting transfers between devices: none -> 7.93 us  [swap(): lax.ppermute(values, axis, [(i, i ^ distance) for i in range(lax.axis_siz...]
    dot_general x2, matrix products: 7.89 us -> 14.2 us  [contract_first(): lax.dot_general(left, right, (((0,), (0,)), ((), ())), preferred_element_...]
    broadcast_in_dim x0 -> x1, local copies, waits for them, and re-layouts: none -> 3.42 us  [gather_tokens(): everyone = jnp.zeros((lax.axis_size('rows') * count, features), own.dtype)]
    convert_element_type x1 -> x0, other arithmetic: 3.24 us -> none  [normed(): (values * lax.rsqrt(variance + 1e-06) * (1.0 + pre_gain)).astype(jnp.bflo...]
  transfers between devices with their start and end apart: 1 -> 9, of which waited for: 1 -> 2; matrix products, arithmetic and copies ran while one was open for 15% -> 22% of each run, Pallas kernels for 0% -> 0%
where the time goes in v2:
time: 178 us
  Pallas kernels  84.5 us (47%)
  matrix products  55.1 us (31%)
  local copies, waits for them, and re-layouts  15.1 us (8%)
  waiting for transfers between devices  9.05 us (5%)
  starting transfers between devices  7.93 us (4%)
  other arithmetic  5.22 us (3%)
    pallas_call x1, Pallas kernels, total_over_devices(): pl.pallas_call(functools.partial(total_kernel, z_size), out_shape=jax.Sha...  84.5 us
    dot_general x1, matrix products, on_device(): target = jnp.dot(hidden_units, w_down, preferred_element_type=jnp.float32)  18.6 us
    dot_general x2, matrix products, contract_first(): lax.dot_general(left, right, (((0,), (0,)), ((), ())), preferred_element_...  14.2 us
    dynamic_update_slice x9, local copies, waits for them, and re-layouts, place(): return lax.dynamic_update_slice_in_dim(everyone, values, start, 0)  10.4 us
    dot_general x1, matrix products, on_device(): gate_proj = jnp.dot(normal_in, w_gate, preferred_element_type=jnp.float32)  9.91 us
    ppermute x9, waiting for transfers between devices, swap(): lax.ppermute(values, axis, [(i, i ^ distance) for i in range(lax.axis_siz...  9.05 us
    ppermute x9, starting transfers between devices, swap(): lax.ppermute(values, axis, [(i, i ^ distance) for i in range(lax.axis_siz...  7.93 us
    dot_general x1, matrix products, on_device(): jnp.dot(tok_rows, w_enc, preferred_element_type=jnp.float32)  5.78 us
  transfers between devices with their start and end apart: 9, of which 2 were waited for; matrix products, arithmetic and copies ran while one was open for 22% of the time, Pallas kernels for 0%

profile of v2, /device:TPU:0, one launch (start us, length us, event | category | flops | bytes accessed | tf_op | source)
XLA Modules:
  0.0 177.7 jit_solution(11349068476319612622)
XLA Ops:
  0.6 0.0 copy-start
  0.7 0.9 broadcast_add_fusion
  1.5 1.9 %fusion.2 = f32[256]{0:T(256)S(1)} fusion(bf16[256,3584]{1,0:T(8,128)(2,1)} %param.9), kind=kLoop, calls=%fused_computation.7 | loop fusion | flops 2752256 | bytes 1836032 | tf_op jit(solution)/shard_map/reduce_sum | solution.py:16
  3.5 0.0 copy-start.2
  3.5 3.4 %broadcast_in_dim.34 = bf16[1024,3584]{1,0:T(8,128)(2,1)} broadcast(bf16[]{:T(256)} %constant.21.clone.1), dimensions={} | broadcast | bytes 7340034 | tf_op jit(solution)/shard_map/broadcast_in_dim | solution.py:231
  6.9 0.0 copy-done.2
  6.9 2.4 %constant_dynamic-update-slice_fusion.9 = (bf16[1024,3584]{1,0:T(8,128)(2,1)}, bf16[256,3584]{1,0:T(8,128)(2,1)}) fusion(bf16[1024,3584]{1,0:T(8,128)(2,1)} %broadcast_in_dim.34, s32[]{:T(128)S(6)} %select_n.48, f32[3584]{0:T(1024)S(1)} %broadcast_add_fusion, f32[256]{0:T(256)S(1)} %add_rsqrt_fusion, bf16[256,3584]{1,0:T(8,128)(2,1)S(1)} %copy-done.2), kind=kLoop, calls=%fused_computation.39 | loop fusion | flops 3670016 | bytes 5520388 | tf_op jit(solution)/shard_map/dynamic_update_slice | solution.py:234
  9.3 0.4 collective-permute-start
  9.7 1.2 constant_dynamic-slice_fusion
  10.9 2.6 %collective-permute-start.1 = (bf16[64,3584]{1,0:T(8,128)(2,1)S(1)}, bf16[64,3584]{1,0:T(8,128)(2,1)S(1)}, u32[]{:S(2)}, u32[]{:S(2)}) collective-permute-start(bf16[64,3584]{1,0:T(8,128)(2,1)S(1)} %get-tuple-element.5), channel_id=1, source_target_pairs={{0,16},{8,24},{16,0},{24,8},{1,17},{9,25},{17,1},{25,9},{2,18},{10... | collective-permute-start | bytes 1376264 | tf_op jit(solution)/shard_map/ppermute | solution.py:223
  13.5 0.1 collective-permute-start.5
  13.6 9.9 %fusion.22 = f32[256,1792]{1,0:T(8,128)} fusion(bf16[256,3584]{1,0:T(8,128)(2,1)} %get-tuple-element.3, bf16[3584,1792]{1,0:T(8,128)(2,1)} %param.11), kind=kOutput, calls=%fused_computation.46 | convolution fusion | flops 3288334336 | bytes 16515072 | tf_op jit(solution)/shard_map/dot_general | solution.py:260
  23.5 0.0 copy-start.6
  23.5 0.0 copy-start.4
  23.5 1.4 collective-permute-done.1
  24.9 2.0 %collective-permute-start.2 = (bf16[64,3584]{1,0:T(8,128)(2,1)S(1)}, bf16[64,3584]{1,0:T(8,128)(2,1)}, u32[]{:S(2)}, u32[]{:S(2)}) collective-permute-start(bf16[64,3584]{1,0:T(8,128)(2,1)S(1)} %collective-permute-done.1), channel_id=1, source_target_pairs={{0,1},{1,0},{2,3},{3,2},{4,5},{5,4},{6,7},{7,6},{8,9},{9,8},{10,11... | collective-permute-start | bytes 1376264 | tf_op jit(solution)/shard_map/ppermute | solution.py:223
  26.9 7.7 %collective-permute-done.5 = bf16[64,3584]{1,0:T(8,128)(2,1)S(1)} collective-permute-done((bf16[64,3584]{1,0:T(8,128)(2,1)S(1)}, bf16[64,3584]{1,0:T(8,128)(2,1)S(1)}, u32[]{:S(2)}, u32[]{:S(2)}) %collective-permute-start.5) | collective-permute-done | bytes 458784 | tf_op jit(solution)/shard_map/ppermute | solution.py:223
  34.5 1.8 %collective-permute-start.6 = (bf16[64,3584]{1,0:T(8,128)(2,1)S(1)}, bf16[64,3584]{1,0:T(8,128)(2,1)S(1)}, u32[]{:S(2)}, u32[]{:S(2)}) collective-permute-start(bf16[64,3584]{1,0:T(8,128)(2,1)S(1)} %collective-permute-done.5), channel_id=1, source_target_pairs={{0,1},{1,0},{2,3},{3,2},{4,5},{5,4},{6,7},{7,6},{8,9},{9,8},{10,11... | collective-permute-start | bytes 1376264 | tf_op jit(solution)/shard_map/ppermute | solution.py:223
  36.3 18.6 %fusion.16 = f32[256,3584]{1,0:T(8,128)} fusion(bf16[1792,3584]{1,0:T(8,128)(2,1)} %param.13, bf16[256,3584]{1,0:T(8,128)(2,1)} %get-tuple-element.3, bf16[3584,1792]{1,0:T(8,128)(2,1)} %param.12, f32[256,1792]{1,0:T(8,128)} %fusion.22), kind=kOutput, calls=%fused_computation.26 | convolution fusion | flops 6581256192 | bytes 33030144 | tf_op jit(solution)/shard_map/dot_general | solution.py:263
  54.9 0.0 copy-done.6
  54.9 0.1 broadcast_in_dim.35
  55.0 0.0 copy-done.4
  55.1 0.0 copy-start.5
  55.1 0.1 collective-permute-start.3
  55.2 0.5 collective-permute-start.7
  55.7 0.0 collective-permute-done.2
  55.7 0.1 collective-permute-start.4
  55.7 0.0 collective-permute-done.6
  55.7 0.4 collective-permute-start.8
  56.2 0.0 collective-permute-done
  56.2 2.9 %constant_dynamic-update-slice_fusion.8 = bf16[1024,3584]{1,0:T(8,128)(2,1)} fusion(bf16[1024,3584]{1,0:T(8,128)(2,1)} %get-tuple-element.2, bf16[256,3584]{1,0:T(8,128)(2,1)} %collective-permute-done, s32[]{:T(128)S(6)} %select_n.49), kind=kLoop, calls=%fused_computation.38 | loop fusion | bytes 3670020 | tf_op jit(solution)/shard_map/dynamic_update_slice | solution.py:234
  59.0 0.8 constant_dynamic-update-slice_fusion.7
  59.9 1.8 %constant_dynamic-update-slice_fusion.6 = bf16[1024,3584]{1,0:T(8,128)(2,1)} fusion(bf16[1024,3584]{1,0:T(8,128)(2,1)} %constant_dynamic-update-slice_fusion.7, bf16[64,3584]{1,0:T(8,128)(2,1)} %collective-permute-done.2, s32[]{:T(128)S(6)} %select_n.53), kind=kLoop, calls=%fused_computation.35 | loop fusion | bytes 917508 | tf_op jit(solution)/shard_map/dynamic_update_slice | solution.py:234
  61.7 0.0 collective-permute-done.3
  61.7 0.8 constant_dynamic-update-slice_fusion.5
  62.5 0.0 collective-permute-done.4
  62.5 0.8 constant_dynamic-update-slice_fusion.4
  63.3 0.8 constant_dynamic-update-slice_fusion.3
  64.1 0.8 constant_dynamic-update-slice_fusion.2
  64.9 0.0 collective-permute-done.7
  64.9 0.8 constant_dynamic-update-slice_fusion.1
  65.8 0.0 copy-start.3
  65.8 0.0 collective-permute-done.8
  65.8 0.8 constant_dynamic-update-slice_fusion
  66.6 0.0 copy-done.5
  66.6 5.8 %fusion.14 = f32[1024,256]{1,0:T(8,128)S(1)} fusion(bf16[1024,3584]{1,0:T(8,128)(2,1)} %constant_dynamic-update-slice_fusion, bf16[3584,256]{1,0:T(8,128)(2,1)S(1)} %copy-done.5, f32[256]{0:T(256)S(1)} %convert_element_type.23), kind=kOutput, calls=%fused_computation.23 | convolution fusion | flops 1879572480 | bytes 10224640 | tf_op jit(solution)/shard_map/dot_general | solution.py:268
  72.4 0.0 copy-done
  72.4 0.0 copy-done.3
  72.4 4.5 %fusion.1.part_ref = bf16[1024,3584]{1,0:T(8,128)(2,1)} fusion(bf16[256,3584]{1,0:T(8,128)(2,1)S(1)} %copy-done, f32[256,3584]{1,0:T(8,128)S(1)} %copy-done.3, pred[1024]{0:T(1024)(128)(4,1)S(1)} %broadcast_in_dim.36, f32[1024,256]{1,0:T(8,128)S(1)} %fusion.14), kind=kOutput, calls=%fused_computation.2 | convolution fusion | flops 1890582528 | bytes 13894656 | tf_op jit(solution)/shard_map/dot_general | solution.py:273
  76.9 84.5 %shard_map.104 = bf16[1024,3584]{1,0:T(8,128)(2,1)} custom-call(bf16[1024,3584]{1,0:T(8,128)(2,1)} %fusion.1.part_ref, f32[1,3584]{1,0:T(1,128)S(1)} %reshape.26.bias_ref), custom_call_target="tpu_custom_call" | custom-call | tf_op jit(solution)/shard_map/pallas_call | solution.py:200
  161.4 0.0 copy-start.1
  161.4 7.2 %convolution_multiply_fusion = f32[256,3584]{1,0:T(8,128)} fusion(bf16[1024,3584]{1,0:T(8,128)(2,1)} %shard_map.104, f32[1024,256]{1,0:T(8,128)S(1)} %fusion.14), kind=kOutput, calls=%fused_computation.3 | convolution fusion | flops 1880489984 | bytes 12058624 | tf_op jit(solution)/shard_map/dot_general | solution.py:21
  168.6 0.0 copy-done.1
  168.6 2.1 %fusion.15 = bf16[1024,256]{1,0:T(8,128)(2,1)S(1)} fusion(f32[1024,256]{1,0:T(8,128)S(1)} %fusion.14, bf16[1024,3584]{1,0:T(8,128)(2,1)S(1)} %copy-done.1, bf16[256,3584]{1,0:T(8,128)(2,1)S(1)} %copy-done), kind=kOutput, calls=%fused_computation.24 | convolution fusion | flops 1879834624 | bytes 10747904 | tf_op jit(solution)/shard_map/dot_general | solution.py:27
  170.7 7.0 %convolution_multiply_fusion.1 = f32[3584,256]{1,0:T(8,128)} fusion(bf16[1024,3584]{1,0:T(8,128)(2,1)} %constant_dynamic-update-slice_fusion, bf16[1024,256]{1,0:T(8,128)(2,1)S(1)} %fusion.15), kind=kOutput, calls=%fused_computation.4 | convolution fusion | flops 1879965696 | bytes 11534336 | tf_op jit(solution)/shard_map/dot_general | solution.py:21
  (5 shorter events, 0.0 us)
Async XLA Ops:
  0.6 71.7 %copy-start = (bf16[256,3584]{1,0:T(8,128)(2,1)S(1)}, bf16[256,3584]{1,0:T(8,128)(2,1)}, u32[]{:S(2)}) copy-start(bf16[256,3584]{1,0:T(8,128)(2,1)} %param.16) | copy-start | bytes 5505028
  3.5 3.4 %copy-start.2 = (bf16[256,3584]{1,0:T(8,128)(2,1)S(1)}, bf16[256,3584]{1,0:T(8,128)(2,1)}, u32[]{:S(2)}) copy-start(bf16[256,3584]{1,0:T(8,128)(2,1)} %param.9) | copy-start | bytes 5505028
  9.3 46.9 %collective-permute-start = (bf16[256,3584]{1,0:T(8,128)(2,1)}, bf16[256,3584]{1,0:T(8,128)(2,1)}, u32[]{:S(2)}, u32[]{:S(2)}) collective-permute-start(bf16[256,3584]{1,0:T(8,128)(2,1)} %get-tuple-element.3), channel_id=1, source_target_pairs={{0,8},{8,0},{16,24},{24,16},{1,9},{9,1},{17,25},{25,17},{2,10},{10... | collective-permute-start | bytes 5505032 | tf_op jit(solution)/shard_map/ppermute | solution.py:223
  10.9 13.9 %collective-permute-start.1 = (bf16[64,3584]{1,0:T(8,128)(2,1)S(1)}, bf16[64,3584]{1,0:T(8,128)(2,1)S(1)}, u32[]{:S(2)}, u32[]{:S(2)}) collective-permute-start(bf16[64,3584]{1,0:T(8,128)(2,1)S(1)} %get-tuple-element.5), channel_id=1, source_target_pairs={{0,16},{8,24},{16,0},{24,8},{1,17},{9,25},{17,1},{25,9},{2,18},{10... | collective-permute-start | bytes 1376264 | tf_op jit(solution)/shard_map/ppermute | solution.py:223
  13.5 21.0 %collective-permute-start.5 = (bf16[64,3584]{1,0:T(8,128)(2,1)S(1)}, bf16[64,3584]{1,0:T(8,128)(2,1)S(1)}, u32[]{:S(2)}, u32[]{:S(2)}) collective-permute-start(bf16[64,3584]{1,0:T(8,128)(2,1)S(1)} %get-tuple-element.4), channel_id=1, source_target_pairs={{0,16},{8,24},{16,0},{24,8},{1,17},{9,25},{17,1},{25,9},{2,18},{10... | collective-permute-start | bytes 1376264 | tf_op jit(solution)/shard_map/ppermute | solution.py:223
  23.5 31.4 %copy-start.6 = (bf16[256]{0:T(256)(128)(2,1)S(1)}, bf16[256]{0:T(256)(128)(2,1)}, u32[]{:S(2)}) copy-start(bf16[256]{0:T(256)(128)(2,1)} %param.15) | copy-start | bytes 1540
  23.5 31.5 %copy-start.4 = (f32[3584]{0:T(1024)S(1)}, f32[3584]{0:T(1024)}, u32[]{:S(2)}) copy-start(f32[3584]{0:T(1024)} %param.17) | copy-start | bytes 43012
  24.9 30.8 %collective-permute-start.2 = (bf16[64,3584]{1,0:T(8,128)(2,1)S(1)}, bf16[64,3584]{1,0:T(8,128)(2,1)}, u32[]{:S(2)}, u32[]{:S(2)}) collective-permute-start(bf16[64,3584]{1,0:T(8,128)(2,1)S(1)} %collective-permute-done.1), channel_id=1, source_target_pairs={{0,1},{1,0},{2,3},{3,2},{4,5},{5,4},{6,7},{7,6},{8,9},{9,8},{10,11... | collective-permute-start | bytes 1376264 | tf_op jit(solution)/shard_map/ppermute | solution.py:223
  34.5 21.2 %collective-permute-start.6 = (bf16[64,3584]{1,0:T(8,128)(2,1)S(1)}, bf16[64,3584]{1,0:T(8,128)(2,1)S(1)}, u32[]{:S(2)}, u32[]{:S(2)}) collective-permute-start(bf16[64,3584]{1,0:T(8,128)(2,1)S(1)} %collective-permute-done.5), channel_id=1, source_target_pairs={{0,1},{1,0},{2,3},{3,2},{4,5},{5,4},{6,7},{7,6},{8,9},{9,8},{10,11... | collective-permute-start | bytes 1376264 | tf_op jit(solution)/shard_map/ppermute | solution.py:223
  55.1 11.5 %copy-start.5 = (bf16[3584,256]{1,0:T(8,128)(2,1)S(1)}, bf16[3584,256]{1,0:T(8,128)(2,1)}, u32[]{:S(2)}) copy-start(bf16[3584,256]{1,0:T(8,128)(2,1)} %param.14) | copy-start | bytes 5505028
  55.1 6.6 %collective-permute-start.3 = (bf16[64,3584]{1,0:T(8,128)(2,1)S(1)}, bf16[64,3584]{1,0:T(8,128)(2,1)S(1)}, u32[]{:S(2)}, u32[]{:S(2)}) collective-permute-start(bf16[64,3584]{1,0:T(8,128)(2,1)S(1)} %collective-permute-done.1), channel_id=1, source_target_pairs={{0,8},{8,0},{16,24},{24,16},{1,9},{9,1},{17,25},{25,17},{2,10},{10... | collective-permute-start | bytes 1376264 | tf_op jit(solution)/shard_map/ppermute | solution.py:223
  55.2 9.8 %collective-permute-start.7 = (bf16[64,3584]{1,0:T(8,128)(2,1)S(1)}, bf16[64,3584]{1,0:T(8,128)(2,1)S(1)}, u32[]{:S(2)}, u32[]{:S(2)}) collective-permute-start(bf16[64,3584]{1,0:T(8,128)(2,1)S(1)} %collective-permute-done.5), channel_id=1, source_target_pairs={{0,8},{8,0},{16,24},{24,16},{1,9},{9,1},{17,25},{25,17},{2,10},{10... | collective-permute-start | bytes 1376264 | tf_op jit(solution)/shard_map/ppermute | solution.py:223
  55.7 6.8 %collective-permute-start.4 = (bf16[64,3584]{1,0:T(8,128)(2,1)}, bf16[64,3584]{1,0:T(8,128)(2,1)S(1)}, u32[]{:S(2)}, u32[]{:S(2)}) collective-permute-start(bf16[64,3584]{1,0:T(8,128)(2,1)} %collective-permute-done.2), channel_id=1, source_target_pairs={{0,8},{8,0},{16,24},{24,16},{1,9},{9,1},{17,25},{25,17},{2,10},{10... | collective-permute-start | bytes 1376264 | tf_op jit(solution)/shard_map/ppermute | solution.py:223
  55.7 10.0 %collective-permute-start.8 = (bf16[64,3584]{1,0:T(8,128)(2,1)S(1)}, bf16[64,3584]{1,0:T(8,128)(2,1)S(1)}, u32[]{:S(2)}, u32[]{:S(2)}) collective-permute-start(bf16[64,3584]{1,0:T(8,128)(2,1)S(1)} %collective-permute-done.6), channel_id=1, source_target_pairs={{0,8},{8,0},{16,24},{24,16},{1,9},{9,1},{17,25},{25,17},{2,10},{10... | collective-permute-start | bytes 1376264 | tf_op jit(solution)/shard_map/ppermute | solution.py:223
  65.8 6.6 %copy-start.3 = (f32[256,3584]{1,0:T(8,128)S(1)}, f32[256,3584]{1,0:T(8,128)}, u32[]{:S(2)}) copy-start(f32[256,3584]{1,0:T(8,128)} %fusion.16) | copy-start | bytes 11010052
  161.4 7.2 %copy-start.1 = (bf16[1024,3584]{1,0:T(8,128)(2,1)S(1)}, bf16[1024,3584]{1,0:T(8,128)(2,1)}, u32[]{:S(2)}) copy-start(bf16[1024,3584]{1,0:T(8,128)(2,1)} %shard_map.104) | copy-start | bytes 22020100

commit v3 on v2

--- a/solution.py
+++ b/solution.py
@@ -219,49 +219,179 @@
     )(part, bias)
 
 
-def swap(values, axis, distance):
-    return lax.ppermute(values, axis, [(i, i ^ distance) for i in range(lax.axis_size(axis))])
-
-
-def gather_tokens(own):
+PIECES = 4
+
+
+def widest(size, options):
+    return next(w for w in options if size % w == 0)
+
+
+def mlp_kernel(
+    own_ref, gate_ref, up_ref, down_ref, tok_ref, target_ref,
+    hidden, gates, ups, downs, load_sem, own_sem, send_sem, recv_sem,
+):
+    count, features = own_ref.shape
+    row, hid = lax.axis_index("rows"), lax.axis_index("hidden")
+    x, core, z, y = row // 2, row % 2, hid // 2, hid % 2
+    across = (1 - x) * 2 + core
+    core_peer = {"rows": x * 2 + (1 - core), "hidden": hid}
+    x_peer = {"rows": across, "hidden": hid}
+    y_peer = {"rows": row, "hidden": z * 2 + (1 - y)}
+    barrier = pltpu.get_barrier_semaphore()
+    for peer in (core_peer, x_peer, y_peer):
+        pl.semaphore_signal(barrier, inc=1, device_id=peer, device_id_type=pl.DeviceIdType.MESH)
+    pl.semaphore_wait(barrier, 3)
+
+    half = count // 2
+    size = half // PIECES
+
+    def copy(at, src, dst, peer):
+        return pltpu.make_async_remote_copy(
+            src_ref=src, dst_ref=dst, send_sem=send_sem.at[at], recv_sem=recv_sem.at[at],
+            device_id=peer, device_id_type=pl.DeviceIdType.MESH,
+        )
+
+    def tok(start, rows):
+        return tok_ref.at[pl.ds(pl.multiple_of(start, rows), rows), :]
+
+    mine = tok(row * count, count)
+    place = pltpu.make_async_copy(own_ref, mine, own_sem)
+    to_core = copy(0, own_ref, mine, core_peer)
+    over_x, over_y, core_x, core_y = [], [], [], []
+    for i in range(PIECES):
+        here = y * half + i * size
+        there = (1 - y) * half + i * size
+        piece = own_ref.at[pl.ds(pl.multiple_of(here, size), size), :]
+        over_x.append(copy(1 + i, piece, tok(row * count + here, size), x_peer))
+        got = tok(across * count + here, size)
+        far = tok(across * count + there, size)
+        over_y.append(copy(1 + PIECES + i, got, got, y_peer))
+        core_x.append(copy(1 + 2 * PIECES + i, got, got, core_peer))
+        core_y.append(copy(1 + 3 * PIECES + i, far, far, core_peer))
+
+    for c in over_x:
+        c.start()
+    to_core.start()
+    place.start()
+
+    def took_x(i):
+        over_x[i].wait_recv()
+        over_y[i].start()
+        core_x[i].start()
+
+    def took_y(i):
+        over_y[i].wait_recv()
+        core_y[i].start()
+
+    width, down_width = gates.shape[2], downs.shape[2]
+    steps, down_steps = gate_ref.shape[1] // width, features // down_width
+
+    def tile(i, width, count):
+        return pl.ds(0 if count == 1 else pl.multiple_of(i * width, width), width)
+
+    def loads(i):
+        slot = lax.rem(i, 2)
+        cols = tile(i, width, steps)
+        return (
+            pltpu.make_async_copy(gate_ref.at[:, cols], gates.at[slot], load_sem.at[slot]),
+            pltpu.make_async_copy(up_ref.at[:, cols], ups.at[slot], load_sem.at[2 + slot]),
+        )
+
+    def down_loads(i):
+        slot = lax.rem(i, 2)
+        cols = pl.ds(pl.multiple_of(i * down_width, down_width), down_width)
+        return (pltpu.make_async_copy(down_ref.at[:, cols], downs.at[slot], load_sem.at[4 + slot]),)
+
+    def start(copies):
+        for c in copies:
+            c.start()
+
+    def gate_step(i, carry):
+        @pl.when(i + 1 < steps)
+        def _():
+            start(loads(i + 1))
+
+        for c in loads(i):
+            c.wait()
+        slot = lax.rem(i, 2)
+        gate = jnp.dot(own_ref[...], gates[slot], preferred_element_type=jnp.float32)
+        up = jnp.dot(own_ref[...], ups[slot], preferred_element_type=jnp.float32)
+        hidden[:, tile(i, width, steps)] = (
+            jax.nn.gelu(gate, approximate=True) * up
+        ).astype(jnp.bfloat16)
+        return carry
+
+    def down_step(i, carry):
+        @pl.when(i + 1 < down_steps)
+        def _():
+            start(down_loads(i + 1))
+
+        for c in down_loads(i):
+            c.wait()
+        target_ref[:, pl.ds(pl.multiple_of(i * down_width, down_width), down_width)] = jnp.dot(
+            hidden[...], downs[lax.rem(i, 2)], preferred_element_type=jnp.float32
+        )
+        return carry
+
+    start(loads(0))
+    start(down_loads(0))
+    done = 0
+    for i in range(PIECES):
+        until = min(steps, 2 * (i + 1))
+        lax.fori_loop(done, until, gate_step, 0)
+        done = until
+        took_x(i)
+        if i:
+            took_y(i - 1)
+    lax.fori_loop(done, steps, gate_step, 0)
+    middle = (down_steps * 2) // 3
+    lax.fori_loop(0, middle, down_step, 0)
+    took_y(PIECES - 1)
+    lax.fori_loop(middle, down_steps, down_step, 0)
+
+    place.wait()
+    to_core.wait_recv()
+    for c in core_x + core_y:
+        c.wait_recv()
+    for c in [to_core] + over_x + over_y + core_x + core_y:
+        c.wait_send()
+
+
+def gather_and_mlp(own, w_gate, w_up, w_down):
     count, features = own.shape
-    row, y = lax.axis_index("rows"), lax.axis_index("hidden") % 2
-    pieces = 2
-    size = count // (2 * pieces)
-    everyone = jnp.zeros((lax.axis_size("rows") * count, features), own.dtype)
-
-    def place(everyone, values, start):
-        return lax.dynamic_update_slice_in_dim(everyone, values, start, 0)
-
-    over_x = [
-        swap(lax.dynamic_slice_in_dim(own, y * (count // 2) + i * size, size, 0), "rows", 2)
-        for i in range(pieces)
-    ]
-    over_y = [swap(values, "hidden", 1) for values in over_x]
-    on_chip = swap(own, "rows", 1)
-    everyone = place(everyone, own, row * count)
-    everyone = place(everyone, on_chip, (row ^ 1) * count)
-    across = (row ^ 2) * count
-    far = [swap(values, "rows", 1) for values in over_x + over_y]
-    near_far = (row ^ 3) * count
-    for i in range(pieces):
-        here = y * (count // 2) + i * size
-        there = (1 - y) * (count // 2) + i * size
-        everyone = place(everyone, over_x[i], across + here)
-        everyone = place(everyone, over_y[i], across + there)
-        everyone = place(everyone, far[i], near_far + here)
-        everyone = place(everyone, far[pieces + i], near_far + there)
-    return everyone
+    units = w_gate.shape[1]
+    width = widest(units, (256, 128, units))
+    down_width = widest(features, (512, 256, 128))
+    bf = jnp.bfloat16
+    copies = 1 + 4 * PIECES
+    vmem, anywhere = pl.BlockSpec(memory_space=pltpu.VMEM), pl.BlockSpec(memory_space=pl.ANY)
+    return pl.pallas_call(
+        mlp_kernel,
+        out_shape=(
+            jax.ShapeDtypeStruct((lax.axis_size("rows") * count, features), bf),
+            jax.ShapeDtypeStruct((count, features), jnp.float32),
+        ),
+        in_specs=[vmem, anywhere, anywhere, anywhere],
+        out_specs=(vmem, vmem),
+        scratch_shapes=[
+            pltpu.VMEM((count, units), bf),
+            pltpu.VMEM((2, features, width), bf),
+            pltpu.VMEM((2, features, width), bf),
+            pltpu.VMEM((2, units, down_width), bf),
+            pltpu.SemaphoreType.DMA((6,)),
+            pltpu.SemaphoreType.DMA,
+            pltpu.SemaphoreType.DMA((copies,)),
+            pltpu.SemaphoreType.DMA((copies,)),
+        ],
+        compiler_params=pltpu.CompilerParams(
+            collective_id=1, has_side_effects=True, vmem_limit_bytes=48 * 1024 * 1024
+        ),
+    )(own, w_gate, w_up, w_down)
 
 
 def on_device(z_size, resid_stream, pre_gain, w_gate, w_up, w_down, w_enc, b_enc, w_dec, b_dec):
     normal_in = normed(resid_stream, pre_gain)
-    tok_rows = gather_tokens(normal_in)
-    gate_proj = jnp.dot(normal_in, w_gate, preferred_element_type=jnp.float32)
-    up_proj = jnp.dot(normal_in, w_up, preferred_element_type=jnp.float32)
-    hidden_units = (jax.nn.gelu(gate_proj, approximate=True) * up_proj).astype(jnp.bfloat16)
-    target = jnp.dot(hidden_units, w_down, preferred_element_type=jnp.float32)
-
+    tok_rows, target = gather_and_mlp(normal_in, w_gate, w_up, w_down)
     row_size = lax.axis_size("rows")
     own_tokens, features = normal_in.shape
     factor = 1.0 / math.sqrt(own_tokens * row_size)

time: 178 us -> 151 us (0.85)
  Pallas kernels: 84.5 us -> 120 us
  matrix products: 55.1 us -> 22.6 us
  local copies, waits for them, and re-layouts: 15.1 us -> 0.85 us
  waiting for transfers between devices: 9.05 us -> 0 us
  starting transfers between devices: 7.93 us -> 0 us
    pallas_call x0 -> x1, Pallas kernels: none -> 37 us  [gather_and_mlp(): pl.pallas_call(mlp_kernel, out_shape=(jax.ShapeDtypeStruct((lax.axis_size...]
    dot_general x2 -> x0, matrix products: 28.5 us -> none  [the longest x1 18.6 us: on_device(): target = jnp.dot(hidden_units, w_down, preferred_element_type=jnp.float32)]
    dynamic_update_slice x9 -> x0, local copies, waits for them, and re-layouts: 10.4 us -> none  [place(): return lax.dynamic_update_slice_in_dim(everyone, values, start, 0)]
    ppermute x9 -> x0, waiting for transfers between devices: 9.05 us -> none  [swap(): lax.ppermute(values, axis, [(i, i ^ distance) for i in range(lax.axis_siz...]
    ppermute x9 -> x0, starting transfers between devices: 7.93 us -> none  [swap(): lax.ppermute(values, axis, [(i, i ^ distance) for i in range(lax.axis_siz...]
    dot_general x2, matrix products: 14.2 us -> 7.89 us  [contract_first(): lax.dot_general(left, right, (((0,), (0,)), ((), ())), preferred_element_...]
    broadcast_in_dim x1 -> x0, local copies, waits for them, and re-layouts: 3.42 us -> none  [gather_tokens(): everyone = jnp.zeros((lax.axis_size('rows') * count, features), own.dtype)]
    dot_general x1, matrix products: 2.08 us -> 5.32 us  [contract_last(): lax.dot_general(left, right, (((1,), (1,)), ((), ())), preferred_element_...]
  transfers between devices with their start and end apart: 9 -> 0, of which waited for: 2 -> 0; matrix products, arithmetic and copies ran while one was open for 22% -> 0% of each run, Pallas kernels for 0% -> 0%
where the time goes in v3:
time: 151 us; the launch traced here: 150 us
  Pallas kernels  120 us (79%)
  matrix products  22.6 us (15%)
  other arithmetic  5.45 us (4%)
    pallas_call x1, Pallas kernels, total_over_devices(): pl.pallas_call(functools.partial(total_kernel, z_size), out_shape=jax.Sha...  83.4 us
    pallas_call x1, Pallas kernels, gather_and_mlp(): pl.pallas_call(mlp_kernel, out_shape=(jax.ShapeDtypeStruct((lax.axis_size...  37 us
    dot_general x2, matrix products, contract_first(): lax.dot_general(left, right, (((0,), (0,)), ((), ())), preferred_element_...  7.89 us
    dot_general x1, matrix products, contract_last(): lax.dot_general(left, right, (((1,), (1,)), ((), ())), preferred_element_...  5.32 us
    dot_general x1, matrix products, on_device(): jnp.dot(tok_rows, w_enc, preferred_element_type=jnp.float32)  5.14 us
    dot_general x1, matrix products, on_device(): recon = jnp.dot(own_latent, w_dec, preferred_element_type=jnp.float32)  4.29 us

profile of v3, /device:TPU:0, one launch (start us, length us, event | category | flops | bytes accessed | tf_op | source)
XLA Modules:
  0.0 150.0 jit_solution(12296706869956084697)
XLA Ops:
  0.6 0.0 copy-start
  0.7 0.1 broadcast_in_dim.31
  0.7 0.8 convert_element_type.20
  1.5 1.9 %fusion.2 = f32[256]{0:T(256)S(1)} fusion(bf16[256,3584]{1,0:T(8,128)(2,1)} %param.9), kind=kLoop, calls=%fused_computation.7 | loop fusion | flops 2752256 | bytes 1836032 | tf_op jit(solution)/shard_map/reduce_sum | solution.py:16
  3.5 0.7 reshape.26.bias_ref
  4.2 0.7 broadcast_add_fusion
  4.9 2.0 %fusion.4.own_ref = bf16[256,3584]{1,0:T(8,128)(2,1)S(1)} fusion(bf16[256,3584]{1,0:T(8,128)(2,1)} %param.9, f32[3584]{0:T(1024)S(1)} %broadcast_add_fusion, f32[256]{0:T(256)S(1)} %add_rsqrt_fusion), kind=kLoop, calls=%fused_computation.9 | loop fusion | flops 3670016 | bytes 3685376 | tf_op jit(solution)/shard_map/convert_element_type | solution.py:17
  6.9 0.0 copy-start.2
  7.0 37.0 %shard_map.104 = (bf16[1024,3584]{1,0:T(8,128)(2,1)}, f32[256,3584]{1,0:T(8,128)S(1)}) custom-call(bf16[256,3584]{1,0:T(8,128)(2,1)S(1)} %fusion.4.own_ref, bf16[3584,1792]{1,0:T(8,128)(2,1)} %gate_ref.1, bf16[3584,1792]{1,0:T(8,128)(2,1)} %up_ref.1, bf16[1792,3584]{1,0:T(8,128)(2,1)} %down_ref.1), custom_call_target="tpu_custom_call" | custom-call | tf_op jit(solution)/shard_map/pallas_call | solution.py:368
  44.0 0.0 copy-done.2
  44.0 5.1 %fusion.6 = f32[1024,256]{1,0:T(8,128)S(1)} fusion(bf16[1024,3584]{1,0:T(8,128)(2,1)} %get-tuple-element.4, bf16[3584,256]{1,0:T(8,128)(2,1)S(1)} %copy-done.2, f32[256]{0:T(256)S(1)} %convert_element_type.20), kind=kOutput, calls=%fused_computation.13 | convolution fusion | flops 1879572480 | bytes 10224640 | tf_op jit(solution)/shard_map/dot_general | solution.py:398
  49.1 0.0 copy-done
  49.1 4.3 %fusion.1.part_ref = bf16[1024,3584]{1,0:T(8,128)(2,1)} fusion(bf16[256,3584]{1,0:T(8,128)(2,1)S(1)} %copy-done, f32[256,3584]{1,0:T(8,128)S(1)} %get-tuple-element.5, pred[1024]{0:T(1024)(128)(4,1)S(1)} %broadcast_in_dim.32, f32[1024,256]{1,0:T(8,128)S(1)} %fusion.6), kind=kOutput, calls=%fused_computation.2 | convolution fusion | flops 1890582528 | bytes 13894656 | tf_op jit(solution)/shard_map/dot_general | solution.py:403
  53.4 83.4 %shard_map.105 = bf16[1024,3584]{1,0:T(8,128)(2,1)} custom-call(bf16[1024,3584]{1,0:T(8,128)(2,1)} %fusion.1.part_ref, f32[1,3584]{1,0:T(1,128)S(1)} %reshape.26.bias_ref), custom_call_target="tpu_custom_call" | custom-call | tf_op jit(solution)/shard_map/pallas_call | solution.py:200
  136.8 0.0 copy-start.1
  136.8 0.0 slice-start
  136.8 5.3 %fusion.7 = bf16[1024,256]{1,0:T(8,128)(2,1)S(1)} fusion(f32[1024,256]{1,0:T(8,128)S(1)} %fusion.6, bf16[1024,3584]{1,0:T(8,128)(2,1)} %shard_map.105, bf16[256,3584]{1,0:T(8,128)(2,1)S(1)} %copy-done), kind=kOutput, calls=%fused_computation.14 | convolution fusion | flops 1879834624 | bytes 10747904 | tf_op jit(solution)/shard_map/dot_general | solution.py:27
  142.1 0.0 copy-done.1
  142.1 0.0 slice-start.1
  142.1 3.9 %convolution_multiply_fusion = f32[256,3584]{1,0:T(8,128)} fusion(bf16[1024,3584]{1,0:T(8,128)(2,1)S(1)} %copy-done.1, f32[1024,256]{1,0:T(8,128)S(1)} %fusion.6), kind=kOutput, calls=%fused_computation.3 | convolution fusion | flops 1880489984 | bytes 12058624 | tf_op jit(solution)/shard_map/dot_general | solution.py:21
  146.1 0.0 slice-done
  146.1 0.0 slice-done.1
  146.1 4.0 %convolution_multiply_fusion.1 = f32[3584,256]{1,0:T(8,128)} fusion(bf16[1024,3584]{1,0:T(8,128)(2,1)S(1)} %bitcast.15, bf16[1024,256]{1,0:T(8,128)(2,1)S(1)} %fusion.7), kind=kOutput, calls=%fused_computation.4 | convolution fusion | flops 1879965696 | bytes 11534336 | tf_op jit(solution)/shard_map/dot_general | solution.py:21
  (4 shorter events, 0.0 us)
Async XLA Ops:
  0.6 48.5 %copy-start = (bf16[256,3584]{1,0:T(8,128)(2,1)S(1)}, bf16[256,3584]{1,0:T(8,128)(2,1)}, u32[]{:S(2)}) copy-start(bf16[256,3584]{1,0:T(8,128)(2,1)} %param.16) | copy-start | bytes 5505028
  6.9 37.0 %copy-start.2 = (bf16[3584,256]{1,0:T(8,128)(2,1)S(1)}, bf16[3584,256]{1,0:T(8,128)(2,1)}, u32[]{:S(2)}) copy-start(bf16[3584,256]{1,0:T(8,128)(2,1)} %param.14) | copy-start | bytes 5505028
  136.8 5.3 %copy-start.1 = (bf16[1024,3584]{1,0:T(8,128)(2,1)S(1)}, bf16[1024,3584]{1,0:T(8,128)(2,1)}, u32[]{:S(2)}) copy-start(bf16[1024,3584]{1,0:T(8,128)(2,1)} %shard_map.105) | copy-start | bytes 22020100
  136.8 9.3 %slice-start = ((s8[7340032]{0:T(1024)(128)(4,1)}), s8[4194304]{0:T(1024)(128)(4,1)S(1)}, s32[]{:S(2)}) async-start(s8[7340032]{0:T(1024)(128)(4,1)} %bitcast.14), calls=%async_computation | async-start | bytes 8388608
  142.1 3.9 %slice-start.1 = ((s8[7340032]{0:T(1024)(128)(4,1)}), s8[3145728]{0:T(1024)(128)(4,1)S(1)}, s32[]{:S(2)}) async-start(s8[7340032]{0:T(1024)(128)(4,1)} %bitcast.14), calls=%async_computation.1 | async-start | bytes 6291456

commit v4 on v3

--- a/solution.py
+++ b/solution.py
@@ -45,10 +45,11 @@
 
 
 def total_kernel(
-    z_size, part_ref, bias_ref, out_ref,
-    core_in, acc0, in1, acc1, in2, acc2, in3, send_sem, recv_sem,
+    z_size, factor, latent_ref, turned_ref, rect_ref, dec_ref, target_ref, bias_ref,
+    dec_grad_ref, slope_ref,
+    part_ref, out_ref, back_prop, core_in, acc0, in1, acc1, in2, acc2, in3, send_sem, recv_sem,
 ):
-    tokens, features = part_ref.shape
+    tokens, features = out_ref.shape
     half_f = features // 2
     groups = groups_of(half_f)
     row, hid = lax.axis_index("rows"), lax.axis_index("hidden")
@@ -94,10 +95,51 @@
         return (x, y, x_peer, y_peer) if g % 2 == 0 else (y, x, y_peer, x_peer)
 
     base = 3 + z_size - 1
-    flying = []
-    for g, (off, width) in enumerate(groups):
-        theirs = pl.ds(pl.multiple_of((1 - core) * half_f + off, LANES), width)
-        flying.append(go([copy(g, 0, part_ref.at[:, theirs], core_in.at[:, pl.ds(off, width)], core_peer)]))
+    flying = [[] for _ in groups]
+    own_tokens = target_ref.shape[0]
+    count = len(groups)
+
+    def pair_cols(pair, side):
+        width = sum(w for _, w in groups[2 * pair : 2 * pair + 2])
+        return pl.ds(pl.multiple_of(side * half_f + 2 * pair * LANES, LANES), width)
+
+    def term(i, cols):
+        product = jnp.dot(
+            latent_ref[pl.ds(i, own_tokens), :], dec_ref[:, cols], preferred_element_type=jnp.float32
+        )
+        return product - jnp.where(i == row * own_tokens, target_ref[:, cols], 0.0)
+
+    def make(pair):
+        if 2 * pair >= count:
+            return
+        cols = pair_cols(pair, 1 - core)
+
+        def fill(i):
+            part_ref[pl.ds(i, own_tokens), cols] = term(i, cols).astype(jnp.bfloat16)
+
+        by_rows(tokens, own_tokens, fill)
+        for g in range(2 * pair, min(2 * pair + 2, count)):
+            off, width = groups[g]
+            theirs = pl.ds(pl.multiple_of((1 - core) * half_f + off, LANES), width)
+            flying[g] = go([
+                copy(g, 0, part_ref.at[:, theirs], core_in.at[:, pl.ds(off, width)], core_peer)
+            ])
+
+    def use(pair, side):
+        cols = pair_cols(pair, side)
+        dec_grad_ref[:, cols] = (
+            jnp.dot(turned_ref[...], out_ref[:, cols], preferred_element_type=jnp.float32) * factor
+        )
+
+        def add(i):
+            rows = pl.ds(i, own_tokens)
+            back_prop[rows, :] += contract_last(out_ref[rows, cols], dec_ref[:, cols])
+
+        by_rows(tokens, own_tokens, add)
+
+    make(0)
+    back_prop[...] = jnp.zeros_like(back_prop)
+    make(1)
 
     def sum_cores(g):
         off, width = groups[g]
@@ -105,12 +147,12 @@
         cols, own = pl.ds(off, width), mine(off, width)
 
         def add(i):
-            rows = pl.ds(i, 128)
-            acc0[rows, cols] = (
-                part_ref[rows, own].astype(jnp.float32) + core_in[rows, cols].astype(jnp.float32)
-            ).astype(jnp.bfloat16)
-
-        by_rows(tokens, 128, add)
+            rows = pl.ds(i, own_tokens)
+            acc0[rows, cols] = (term(i, own) + core_in[rows, cols].astype(jnp.float32)).astype(
+                jnp.bfloat16
+            )
+
+        by_rows(tokens, own_tokens, add)
         return [copy(g, 1, acc0.at[rows_at((1 - b1) * t1, t1), cols], in1.at[:, cols], p1)]
 
     def sum_first(g):
@@ -177,8 +219,8 @@
         return []
 
     work = (sum_cores, sum_first, sum_second, sum_last, give_quarter, give_half, give_core, end)
-    count = len(groups)
-    for step in range((count + 1) // 2 + LAGS[-1]):
+    pairs = (count + 1) // 2
+    for step in range(pairs + LAGS[-1]):
         for stage in (0,) + tuple(range(len(work) - 1, 0, -1)):
             pair = step - LAGS[stage]
             for g in (2 * pair, 2 * pair + 1):
@@ -186,23 +228,39 @@
                     for c in flying[g]:
                         c.wait_recv()
                     flying[g] = go(work[stage](g))
-
+        make(step + 2)
+        for stage, side in ((6, core), (7, 1 - core)):
+            if 0 <= step - LAGS[stage] < pairs:
+                use(step - LAGS[stage], side)
+
+    def slopes(i):
+        rows = pl.ds(i, own_tokens)
+        slope_ref[rows, :] = (back_prop[rows, :] * 2.0 * rect_ref[rows, :]).astype(jnp.bfloat16)
+
+    by_rows(tokens, own_tokens, slopes)
     for c in started:
         c.wait_send()
 
 
-def total_over_devices(part, bias, z_size):
-    tokens, features = part.shape
+def total_and_grads(latent, rect, w_dec, target, bias, z_size, factor):
+    tokens, own_latents = latent.shape
+    features = w_dec.shape[1]
     half_f = features // 2
     stages = 2 * (3 + z_size - 1) * len(groups_of(half_f))
     t1, t2, t3 = tokens // 2, tokens // 4, tokens // (4 * z_size)
     bf = jnp.bfloat16
     return pl.pallas_call(
-        functools.partial(total_kernel, z_size),
-        out_shape=jax.ShapeDtypeStruct((tokens, features), bf),
-        in_specs=[pl.BlockSpec(memory_space=pltpu.VMEM)] * 2,
-        out_specs=pl.BlockSpec(memory_space=pltpu.VMEM),
+        functools.partial(total_kernel, z_size, factor),
+        out_shape=(
+            jax.ShapeDtypeStruct((own_latents, features), jnp.float32),
+            jax.ShapeDtypeStruct((tokens, own_latents), bf),
+        ),
+        in_specs=[pl.BlockSpec(memory_space=pltpu.VMEM)] * 6,
+        out_specs=(pl.BlockSpec(memory_space=pltpu.VMEM),) * 2,
         scratch_shapes=[
+            pltpu.VMEM((tokens, features), bf),
+            pltpu.VMEM((tokens, features), bf),
+            pltpu.VMEM((tokens, own_latents), jnp.float32),
             pltpu.VMEM((tokens, half_f), bf),
             pltpu.VMEM((tokens, half_f), bf),
             pltpu.VMEM((t1, half_f), bf),
@@ -214,9 +272,9 @@
             pltpu.SemaphoreType.DMA((stages,)),
         ],
         compiler_params=pltpu.CompilerParams(
-            collective_id=0, has_side_effects=True, vmem_limit_bytes=48 * 1024 * 1024
+            collective_id=0, has_side_effects=True, vmem_limit_bytes=56 * 1024 * 1024
         ),
-    )(part, bias)
+    )(latent, latent.T, rect, w_dec, target, bias)
 
 
 PIECES = 4
@@ -400,16 +458,10 @@
     )
     own_rect = jnp.maximum(own_pre, 0.0)
     own_latent = (own_rect * own_rect).astype(jnp.bfloat16)
-    recon = jnp.dot(own_latent, w_dec, preferred_element_type=jnp.float32)
-    own_block = (jnp.arange(row_size) == lax.axis_index("rows"))[:, None, None]
-    part = recon.reshape(row_size, own_tokens, features) - jnp.where(own_block, target[None], 0.0)
-    part = part.reshape(row_size * own_tokens, features).astype(jnp.bfloat16)
-    mis_rows = total_over_devices(part, b_dec.reshape(1, features), z_size)
-
-    dec_total = contract_first(own_latent, mis_rows)
-    own_slope = (contract_last(mis_rows, w_dec) * 2.0 * own_rect).astype(jnp.bfloat16)
-    enc_total = contract_first(tok_rows, own_slope)
-    return (enc_total * factor, dec_total * factor)
+    dec_grad, own_slope = total_and_grads(
+        own_latent, own_rect, w_dec, target, b_dec.reshape(1, features), z_size, factor
+    )
+    return (contract_first(tok_rows, own_slope) * factor, dec_grad)
 
 
 def solution(mesh):

time: 151 us -> 153 us (1.013)
  Pallas kernels: 120 us -> 128 us
  matrix products: 22.6 us -> 14.7 us
  local copies, waits for them, and re-layouts: 0.85 us -> 4.21 us
    dot_general x2 -> x0, matrix products: 9.61 us -> none  [the longest x1 5.32 us: contract_last(): lax.dot_general(left, right, (((1,), (1,)), ((), ())), preferred_element_...]
    pallas_call x1, Pallas kernels: 83.4 us -> 90.6 us  [total_and_grads(): pl.pallas_call(functools.partial(total_kernel, z_size, factor), out_shape...]
    dot_general x1, matrix products: 5.14 us -> 7.44 us  [on_device(): jnp.dot(tok_rows, w_enc, preferred_element_type=jnp.float32)]
    unnamed x10 -> x11, local copies, waits for them, and re-layouts: 0.03 us -> 1.87 us
    dot_general x2 -> x1, matrix products: 7.89 us -> 7.23 us  [contract_first(): lax.dot_general(left, right, (((0,), (0,)), ((), ())), preferred_element_...]
where the time goes in v4:
time: 153 us
  Pallas kernels  128 us (84%)
  matrix products  14.7 us (10%)
  other arithmetic  5.47 us (4%)
  local copies, waits for them, and re-layouts  4.21 us (3%)
    pallas_call x1, Pallas kernels, total_and_grads(): pl.pallas_call(functools.partial(total_kernel, z_size, factor), out_shape...  90.6 us
    pallas_call x1, Pallas kernels, gather_and_mlp(): pl.pallas_call(mlp_kernel, out_shape=(jax.ShapeDtypeStruct((lax.axis_size...  37 us
    dot_general x1, matrix products, on_device(): jnp.dot(tok_rows, w_enc, preferred_element_type=jnp.float32)  7.44 us
    dot_general x1, matrix products, contract_first(): lax.dot_general(left, right, (((0,), (0,)), ((), ())), preferred_element_...  7.23 us

profile of v4, /device:TPU:0, one launch (start us, length us, event | category | flops | bytes accessed | tf_op | source)
XLA Modules:
  0.0 152.6 jit_solution(4687171379410680440)
XLA Ops:
  0.6 0.0 copy-start
  0.6 0.8 convert_element_type.16
  1.4 1.9 %fusion = f32[256]{0:T(256)S(1)} fusion(bf16[256,3584]{1,0:T(8,128)(2,1)} %param.9), kind=kLoop, calls=%fused_computation.3 | loop fusion | flops 2752256 | bytes 1836032 | tf_op jit(solution)/shard_map/reduce_sum | solution.py:16
  3.4 1.3 reshape.17.bias_ref
  4.7 0.7 broadcast_add_fusion
  5.4 2.0 %fusion.2.own_ref = bf16[256,3584]{1,0:T(8,128)(2,1)S(1)} fusion(bf16[256,3584]{1,0:T(8,128)(2,1)} %param.9, f32[3584]{0:T(1024)S(1)} %broadcast_add_fusion, f32[256]{0:T(256)S(1)} %add_rsqrt_fusion), kind=kLoop, calls=%fused_computation.5 | loop fusion | flops 3670016 | bytes 3685376 | tf_op jit(solution)/shard_map/convert_element_type | solution.py:17
  7.5 37.0 %shard_map.104 = (bf16[1024,3584]{1,0:T(8,128)(2,1)}, f32[256,3584]{1,0:T(8,128)S(1)}) custom-call(bf16[256,3584]{1,0:T(8,128)(2,1)S(1)} %fusion.2.own_ref, bf16[3584,1792]{1,0:T(8,128)(2,1)} %gate_ref.1, bf16[3584,1792]{1,0:T(8,128)(2,1)} %up_ref.1, bf16[1792,3584]{1,0:T(8,128)(2,1)} %down_ref.1), custom_call_target="tpu_custom_call" | custom-call | tf_op jit(solution)/shard_map/pallas_call | solution.py:426
  44.5 0.0 copy-start.2
  44.5 0.0 copy-done
  44.5 7.4 %multiply_convert_fusion = (bf16[1024,256]{1,0:T(8,128)(2,1)S(1)}, f32[1024,256]{1,0:T(8,128)}) fusion(f32[256]{0:T(256)S(1)} %convert_element_type.16, bf16[1024,3584]{1,0:T(8,128)(2,1)} %get-tuple-element.6, bf16[3584,256]{1,0:T(8,128)(2,1)S(1)} %copy-done), kind=kOutput, calls=%fused_computation.8 | convolution fusion | flops 1880096768 | bytes 10748928 | tf_op jit(solution)/shard_map/dot_general | solution.py:456
  51.9 0.0 copy-done.2
  51.9 0.0 copy-start.4
  51.9 1.0 copy.11.turned_ref
  52.9 0.0 copy-done.4
  52.9 90.6 %shard_map.105 = (f32[256,3584]{1,0:T(8,128)}, bf16[1024,256]{1,0:T(8,128)(2,1)}) custom-call(bf16[1024,256]{1,0:T(8,128)(2,1)} %copy-done.4, bf16[256,1024]{1,0:T(8,128)(2,1)} %copy.11.turned_ref, f32[1024,256]{1,0:T(8,128)} %get-tuple-element.11.rect_ref, bf16[256,3584]{1,0:T(8,128)(2,1)} %dec_ref.1, f32[256,3584]{1,0:T(8,128)} %copy-done.2, ...), custom_call_target="tpu_custom_call" | custom-call | tf_op jit(solution)/shard_map/pallas_call | solution.py:252
  143.5 0.0 copy-start.3
  143.5 0.0 copy-start.1
  143.6 7.2 %convolution_multiply_fusion = f32[3584,256]{1,0:T(8,128)} fusion(bf16[1024,3584]{1,0:T(8,128)(2,1)} %get-tuple-element.6, bf16[1024,256]{1,0:T(8,128)(2,1)} %get-tuple-element.8), kind=kOutput, calls=%fused_computation | convolution fusion | flops 1879965696 | bytes 11534336 | tf_op jit(solution)/shard_map/dot_general | solution.py:21
  150.8 0.0 copy-done.3
  150.8 1.8 %copy.13 = f32[256,3584]{1,0:T(8,128)} copy(f32[256,3584]{1,0:T(8,128)S(1)} %copy-done.3) | data formatting | bytes 7340032
  152.6 0.0 copy-done.1
  (1 shorter events, 0.0 us)
Async XLA Ops:
  0.6 43.8 %copy-start = (bf16[3584,256]{1,0:T(8,128)(2,1)S(1)}, bf16[3584,256]{1,0:T(8,128)(2,1)}, u32[]{:S(2)}) copy-start(bf16[3584,256]{1,0:T(8,128)(2,1)} %param.14) | copy-start | bytes 5505028
  44.5 7.5 %copy-start.2 = (f32[256,3584]{1,0:T(8,128)}, f32[256,3584]{1,0:T(8,128)S(1)}, u32[]{:S(2)}) copy-start(f32[256,3584]{1,0:T(8,128)S(1)} %get-tuple-element.7.target_ref) | copy-start | bytes 11010052
  51.9 1.0 copy-start.4
  143.5 7.3 %copy-start.3 = (f32[256,3584]{1,0:T(8,128)S(1)}, f32[256,3584]{1,0:T(8,128)}, u32[]{:S(2)}) copy-start(f32[256,3584]{1,0:T(8,128)} %get-tuple-element.15) | copy-start | bytes 11010052
  143.5 9.1 %copy-start.1 = (bf16[3584,256]{1,0:T(8,128)(2,1)S(1)}, bf16[3584,256]{1,0:T(8,128)(2,1)}, u32[]{:S(2)}) copy-start(bf16[3584,256]{1,0:T(8,128)(2,1)} %param.14) | copy-start | bytes 5505028

commit v5 on v4

--- a/solution.py
+++ b/solution.py
@@ -41,7 +41,7 @@
     return [(at, LANES) for at in range(0, half, LANES)]
 
 
-LAGS = (0, 2, 3, 4, 5, 6, 8, 9)
+LAGS = (0, 2, 4, 6, 8, 10, 12, 13)
 
 
 def total_kernel(
@@ -272,7 +272,7 @@
             pltpu.SemaphoreType.DMA((stages,)),
         ],
         compiler_params=pltpu.CompilerParams(
-            collective_id=0, has_side_effects=True, vmem_limit_bytes=56 * 1024 * 1024
+            collective_id=0, has_side_effects=True, vmem_limit_bytes=44 * 1024 * 1024
         ),
     )(latent, latent.T, rect, w_dec, target, bias)
 

time: 153 us -> 140 us (0.915)
  Pallas kernels: 128 us -> 119 us
  matrix products: 14.7 us -> 10.4 us
    pallas_call x1, Pallas kernels: 90.6 us -> 81.8 us  [total_and_grads(): pl.pallas_call(functools.partial(total_kernel, z_size, factor), out_shape...]
    dot_general x1, matrix products: 7.23 us -> 3.96 us  [contract_first(): lax.dot_general(left, right, (((0,), (0,)), ((), ())), preferred_element_...]
where the time goes in v5:
time: 140 us
  Pallas kernels  119 us (85%)
  matrix products  10.4 us (7%)
  other arithmetic  5.47 us (4%)
  local copies, waits for them, and re-layouts  4.3 us (3%)
    pallas_call x1, Pallas kernels, total_and_grads(): pl.pallas_call(functools.partial(total_kernel, z_size, factor), out_shape...  81.8 us
    pallas_call x1, Pallas kernels, gather_and_mlp(): pl.pallas_call(mlp_kernel, out_shape=(jax.ShapeDtypeStruct((lax.axis_size...  37 us
    dot_general x1, matrix products, on_device(): jnp.dot(tok_rows, w_enc, preferred_element_type=jnp.float32)  6.47 us
    dot_general x1, matrix products, contract_first(): lax.dot_general(left, right, (((0,), (0,)), ((), ())), preferred_element_...  3.96 us
    unnamed x11, local copies, waits for them, and re-layouts  3.36 us

profile of v5, /device:TPU:0, one launch (start us, length us, event | category | flops | bytes accessed | tf_op | source)
XLA Modules:
  0.0 139.7 jit_solution(2991442871574248566)
XLA Ops:
  0.6 0.0 copy-start
  0.6 0.8 convert_element_type.16
  1.4 1.9 %fusion = f32[256]{0:T(256)S(1)} fusion(bf16[256,3584]{1,0:T(8,128)(2,1)} %param.9), kind=kLoop, calls=%fused_computation.3 | loop fusion | flops 2752256 | bytes 1836032 | tf_op jit(solution)/shard_map/reduce_sum | solution.py:16
  3.4 0.7 reshape.17.bias_ref
  4.1 0.7 broadcast_add_fusion
  4.8 2.0 %fusion.2.own_ref = bf16[256,3584]{1,0:T(8,128)(2,1)S(1)} fusion(bf16[256,3584]{1,0:T(8,128)(2,1)} %param.9, f32[3584]{0:T(1024)S(1)} %broadcast_add_fusion, f32[256]{0:T(256)S(1)} %add_rsqrt_fusion), kind=kLoop, calls=%fused_computation.5 | loop fusion | flops 3670016 | bytes 3685376 | tf_op jit(solution)/shard_map/convert_element_type | solution.py:17
  6.9 37.0 %shard_map.104 = (bf16[1024,3584]{1,0:T(8,128)(2,1)}, f32[256,3584]{1,0:T(8,128)S(1)}) custom-call(bf16[256,3584]{1,0:T(8,128)(2,1)S(1)} %fusion.2.own_ref, bf16[3584,1792]{1,0:T(8,128)(2,1)} %gate_ref.1, bf16[3584,1792]{1,0:T(8,128)(2,1)} %up_ref.1, bf16[1792,3584]{1,0:T(8,128)(2,1)} %down_ref.1), custom_call_target="tpu_custom_call" | custom-call | tf_op jit(solution)/shard_map/pallas_call | solution.py:426
  43.9 0.0 copy-start.2
  43.9 0.0 copy-done
  43.9 6.5 %multiply_convert_fusion = (bf16[1024,256]{1,0:T(8,128)(2,1)S(1)}, f32[1024,256]{1,0:T(8,128)S(1)}) fusion(f32[256]{0:T(256)S(1)} %convert_element_type.16, bf16[1024,3584]{1,0:T(8,128)(2,1)} %get-tuple-element.6, bf16[3584,256]{1,0:T(8,128)(2,1)S(1)} %copy-done), kind=kOutput, calls=%fused_computation.8 | convolution fusion | flops 1880096768 | bytes 10748928 | tf_op jit(solution)/shard_map/dot_general | solution.py:456
  50.3 0.0 copy-done.2
  50.4 0.2 copy.11.turned_ref
  50.6 0.0 copy-start.3
  50.6 1.5 %copy-done.3 = bf16[256,3584]{1,0:T(8,128)(2,1)S(1)} copy-done((bf16[256,3584]{1,0:T(8,128)(2,1)S(1)}, bf16[256,3584]{1,0:T(8,128)(2,1)}, u32[]{:S(2)}) %copy-start.3) | copy-done | bytes 1835032
  52.1 0.0 copy-start.4
  52.1 81.8 %shard_map.105 = (f32[256,3584]{1,0:T(8,128)S(1)}, bf16[1024,256]{1,0:T(8,128)(2,1)S(1)}) custom-call(bf16[1024,256]{1,0:T(8,128)(2,1)S(1)} %get-tuple-element.10.latent_ref, bf16[256,1024]{1,0:T(8,128)(2,1)S(1)} %copy.11.turned_ref, f32[1024,256]{1,0:T(8,128)S(1)} %get-tuple-element.11.rect_ref, bf16[256,3584]{1,0:T(8,128)(2,1)S(1)} %copy-done.3, ...), custom_call_target="tpu_custom_call" | custom-call | tf_op jit(solution)/shard_map/pallas_call | solution.py:252
  133.9 0.0 copy-done.4
  133.9 0.0 copy-start.1
  134.0 4.0 %convolution_multiply_fusion = f32[3584,256]{1,0:T(8,128)} fusion(bf16[1024,3584]{1,0:T(8,128)(2,1)S(1)} %copy-done.4, bf16[1024,256]{1,0:T(8,128)(2,1)S(1)} %get-tuple-element.8), kind=kOutput, calls=%fused_computation | convolution fusion | flops 1879965696 | bytes 11534336 | tf_op jit(solution)/shard_map/dot_general | solution.py:21
  137.9 1.8 %copy.13 = f32[256,3584]{1,0:T(8,128)} copy(f32[256,3584]{1,0:T(8,128)S(1)} %get-tuple-element.15) | data formatting | bytes 7340032
  139.7 0.0 copy-done.1
  (1 shorter events, 0.0 us)
Async XLA Ops:
  0.6 43.2 %copy-start = (bf16[3584,256]{1,0:T(8,128)(2,1)S(1)}, bf16[3584,256]{1,0:T(8,128)(2,1)}, u32[]{:S(2)}) copy-start(bf16[3584,256]{1,0:T(8,128)(2,1)} %param.14) | copy-start | bytes 5505028
  43.9 6.5 %copy-start.2 = (f32[256,3584]{1,0:T(8,128)}, f32[256,3584]{1,0:T(8,128)S(1)}, u32[]{:S(2)}) copy-start(f32[256,3584]{1,0:T(8,128)S(1)} %get-tuple-element.7.target_ref) | copy-start | bytes 11010052
  50.6 1.5 %copy-start.3 = (bf16[256,3584]{1,0:T(8,128)(2,1)S(1)}, bf16[256,3584]{1,0:T(8,128)(2,1)}, u32[]{:S(2)}) copy-start(bf16[256,3584]{1,0:T(8,128)(2,1)} %dec_ref.1) | copy-start | bytes 5505028
  52.1 81.9 %copy-start.4 = (bf16[1024,3584]{1,0:T(8,128)(2,1)S(1)}, bf16[1024,3584]{1,0:T(8,128)(2,1)}, u32[]{:S(2)}) copy-start(bf16[1024,3584]{1,0:T(8,128)(2,1)} %get-tuple-element.6) | copy-start | bytes 22020100
  133.9 5.8 %copy-start.1 = (bf16[3584,256]{1,0:T(8,128)(2,1)S(1)}, bf16[3584,256]{1,0:T(8,128)(2,1)}, u32[]{:S(2)}) copy-start(bf16[3584,256]{1,0:T(8,128)(2,1)} %param.14) | copy-start | bytes 5505028
